TPU v7x, 128 devices: a whole 4x4x4 slice. The times are simulated.
128 devices in a mesh: gz: 32 (over z, x, core), gy: 4 (over y).
Axes of the slice: x: 4, y: 4, z: 4, core: 2. Of those that a mesh axis runs over, the one named last changes fastest.
Arguments:
- excess_warmth: float32 [1536, 6144], P('gz', 'gy'), may hold values from -6 to 6
- pore_moisture: float32 [1536, 6144], P('gz', 'gy'), may hold values from 0.55 to 1
- cement_maturity_degree: float32 [1536, 6144], P('gz', 'gy'), may hold values from 0.05 to 0.85
- parcel_filled_tally: int32 [1536, 48], P('gz', 'gy'), may hold values from 0 to 128
- parcel_keeper_position: int32 [1536, 48], P('gz', 'gy'), may hold values from 0 to 1791, as said below
- layer_pouring_times: int32 [192], replicated, may hold values from 0 to 2000
- voigt_strains_stored: float32 [229376, 8, 128], P(('gz', 'gy')), may hold values from -4 to 4
- micro_tension: float32 [229376, 128], P(('gz', 'gy')), may hold values from 0.5 to 5
Outputs:
- temperature_new: float32 [1536, 6144], P('gz', 'gy')
- humidity_new: float32 [1536, 6144], P('gz', 'gy')
- cement_maturity_after: float32 [1536, 6144], P('gz', 'gy')
- creep_strain: float32 [1536, 6144], P('gz', 'gy')
- voigt_strains_after: float32 [229376, 8, 128], P(('gz', 'gy'))
- micro_tension_after: float32 [229376, 128], P(('gz', 'gy'))
Inputs may be any that keep to these rules, and one draw needn't show every extreme that they name: `parcel_keeper_position`: number the devices gz index * 4 + gy index. The 576 blocks on one device carry distinct values; value // 14 is the device that holds the block's creep state. In every draw one device holds the states of exactly 14 blocks of every device.
All inputs are finite; a program needn't handle non-finite values.
Results may differ from a plain program's by a relative error of at most 0.00002.
Values sent between devices are 32-bit elements; how exact they have to be, the bound alone decides.
No kernel may reach another device: no remote copies, remote signals or barrier semaphores. Data moves between devices by JAX's collectives and lax.ppermute only.
A program may use at most 64 MiB of HBM per device.

v0:
```python
import jax
import jax.numpy as jnp
from jax import lax
from jax.sharding import PartitionSpec as P

NX = 48
PARCEL_SITES = 128
SWEEPS = 3
LIFT = 8


rate_base = 0.05
activation = 0.5
cement_warmth_output = 4.0
desiccation = 0.5
diff_floor = 0.05
humid_scale = 5.0
expansion_factor = 0.5
drying_contraction_factor = 2.0
now_hours = 2400.0
age_scale = 600.0
creep_activation = 0.3
kelvin_amp = 0.15
micro_rate = 0.2
flow_coef = 0.1


def with_halo(cells, sides, width):
    for axis, dim in sides:
        count = lax.axis_size(axis)
        ends = count - 1
        head = lax.slice_in_dim(cells, 0, width, axis=dim)
        tail = lax.slice_in_dim(cells, cells.shape[dim] - width, cells.shape[dim], axis=dim)
        cells = jnp.concatenate(
            [
                lax.ppermute(tail, axis, [(i, (i + 1) % count) for i in range(ends)]),
                cells,
                lax.ppermute(head, axis, [((i + 1) % count, i) for i in range(ends)]),
            ],
            axis=dim,
        )
    return cells


def cement_maturing_speed(field_temp, field_hum, degree):
    humid_term = 7.5 - 7.5 * field_hum
    humid_term = humid_term * humid_term
    return (
        rate_base
        * (1.0 - degree)
        * jnp.exp(activation * field_temp)
        / (1.0 + humid_term * humid_term)
    )


def diffusivity(field_hum):
    ratio = humid_scale * (1.0 - field_hum)
    power = ratio * ratio
    power = power * power
    power = power * power
    power = power * power
    return diff_floor + (1.0 - diff_floor) / (1.0 + power)


def smoothing_iteration(
    present_warmth,
    present_moisture,
    excess_warmth,
    pore_moisture,
    cement_maturity_degree,
    warmth_around,
    moisture_around,
):
    chemical_progress = cement_maturing_speed(
        present_warmth, present_moisture, cement_maturity_degree
    )
    emitted_warmth_total = (
        warmth_around[0]
        + warmth_around[1]
        + warmth_around[2]
        + warmth_around[3]
        + warmth_around[4]
        + warmth_around[5]
    )
    warmth_after = (
        excess_warmth + cement_warmth_output * chemical_progress + emitted_warmth_total
    ) / 7.0
    own_diff = diffusivity(present_moisture)
    conduct = jnp.zeros_like(present_moisture)
    inflow = jnp.zeros_like(present_moisture)
    for neighbour in moisture_around:
        face_diff = 0.5 * (own_diff + diffusivity(neighbour))
        conduct = conduct + face_diff
        inflow = inflow + face_diff * neighbour
    moisture_after = (pore_moisture - desiccation * chemical_progress + inflow) / (1.0 + conduct)
    return (warmth_after, moisture_after)


def viscous_strain_advance(
    loading_tension,
    field_temp,
    field_hum,
    parcel_maturity,
    poured_tally,
    series_prior,
    micro_tension_before,
):
    factor = jnp.exp(creep_activation * field_temp) * (0.1 + 0.9 * field_hum * field_hum)
    lifetimes = 0.1 * 3.0 ** jnp.arange(series_prior.shape[-2]).astype(jnp.float32)
    decays = jnp.exp(-factor[..., None, :] / lifetimes[:, None])
    chain_new = decays * series_prior + kelvin_amp * (1.0 - decays) * loading_tension[..., None, :]
    solidify = jnp.sqrt(age_scale / parcel_maturity) + 0.2
    kelvin_part = solidify * jnp.sum(chain_new - series_prior, axis=-2)
    prestress_next = micro_tension_before / (1.0 + micro_rate * factor * micro_tension_before)
    flow_part = flow_coef * factor * prestress_next * loading_tension
    position = jnp.arange(loading_tension.shape[-1]).astype(jnp.float32)
    placed = position < poured_tally
    series_result = jnp.where(placed[..., None, :], chain_new, series_prior)
    micro_tension_result = jnp.where(placed, prestress_next, micro_tension_before)
    small_change = jnp.where(placed, kelvin_part + flow_part, jnp.zeros_like(loading_tension))
    return (series_result, micro_tension_result, small_change)


def surrounding_entries(stacked, vertical_index):
    local_verticals = stacked.shape[2]
    z_padded = with_halo(stacked, (("gz", 1),), 1)
    y_padded = with_halo(stacked, (("gy", 2),), NX)
    upper_cell = z_padded[:, 2:, :]
    lower_cell = z_padded[:, :-2, :]
    north_cell = y_padded[:, :, 2 * NX : 2 * NX + local_verticals]
    south_cell = y_padded[:, :, 0:local_verticals]
    east_cell = jnp.where(
        vertical_index < NX - 1, jnp.pad(stacked[:, :, 1:], ((0, 0), (0, 0), (0, 1))), 0.0
    )
    west_cell = jnp.where(
        vertical_index > 0, jnp.pad(stacked[:, :, :-1], ((0, 0), (0, 0), (1, 0))), 0.0
    )
    return (upper_cell, lower_cell, north_cell, south_cell, east_cell, west_cell)


def body(
    excess_warmth,
    pore_moisture,
    cement_maturity_degree,
    parcel_filled_tally,
    parcel_keeper_position,
    layer_pouring_times,
    voigt_strains_stored,
    micro_tension,
):
    local_horizontals, local_verticals = excess_warmth.shape
    vertical_index = jnp.arange(local_verticals) % NX
    present_warmth = excess_warmth
    present_moisture = pore_moisture
    for sweep_index in range(SWEEPS):
        flanking_everything = surrounding_entries(
            jnp.stack((present_warmth, present_moisture)), vertical_index
        )
        warmth_around = [volume_site[0] for volume_site in flanking_everything]
        moisture_around = [volume_site[1] for volume_site in flanking_everything]
        present_warmth, present_moisture = smoothing_iteration(
            present_warmth,
            present_moisture,
            excess_warmth,
            pore_moisture,
            cement_maturity_degree,
            warmth_around,
            moisture_around,
        )
    cement_maturity_after = cement_maturity_degree + cement_maturing_speed(
        present_warmth, present_moisture, cement_maturity_degree
    )
    loading_tension = -cement_maturity_after * (
        expansion_factor * present_warmth + drying_contraction_factor * (1.0 - present_moisture)
    )
    parcels_per_line = local_verticals // PARCEL_SITES
    lifts_dev = local_horizontals // LIFT
    start_lift = lax.axis_index("gz") * lifts_dev
    local_times = lax.dynamic_slice_in_dim(layer_pouring_times, start_lift, lifts_dev)
    row_age = now_hours - jnp.repeat(local_times, LIFT).astype(jnp.float32)
    block_ages = jnp.repeat(row_age, parcels_per_line)
    total_slots = voigt_strains_stored.shape[0]
    flat_slot = parcel_keeper_position.reshape(-1)
    payload = jnp.stack(
        (
            loading_tension.reshape(local_horizontals, parcels_per_line, PARCEL_SITES),
            present_warmth.reshape(local_horizontals, parcels_per_line, PARCEL_SITES),
            present_moisture.reshape(local_horizontals, parcels_per_line, PARCEL_SITES),
        ),
        axis=2,
    ).reshape(-1, 3, PARCEL_SITES)
    send_fields = jnp.zeros((total_slots, 3, PARCEL_SITES), jnp.float32).at[flat_slot].set(payload)
    send_count = (
        jnp.zeros((total_slots,), jnp.float32)
        .at[flat_slot]
        .set(parcel_filled_tally.reshape(-1).astype(jnp.float32))
    )
    send_age = jnp.ones((total_slots,), jnp.float32).at[flat_slot].set(block_ages)
    got_fields, got_count, got_age = (
        lax.all_to_all(send_fields, ("gz", "gy"), split_axis=0, concat_axis=0, tiled=True),
        lax.all_to_all(send_count, ("gz", "gy"), split_axis=0, concat_axis=0, tiled=True),
        lax.all_to_all(send_age, ("gz", "gy"), split_axis=0, concat_axis=0, tiled=True),
    )
    series_result, micro_tension_result, small_change = viscous_strain_advance(
        got_fields[:, 0],
        got_fields[:, 1],
        got_fields[:, 2],
        got_age[:, None],
        got_count[:, None],
        voigt_strains_stored,
        micro_tension,
    )
    returned = lax.all_to_all(small_change, ("gz", "gy"), split_axis=0, concat_axis=0, tiled=True)
    creep_cells = returned[flat_slot].reshape(local_horizontals, local_verticals)
    return (
        present_warmth,
        present_moisture,
        cement_maturity_after,
        creep_cells,
        series_result,
        micro_tension_result,
    )


def solution(mesh):
    in_specs = (
        P("gz", "gy"),
        P("gz", "gy"),
        P("gz", "gy"),
        P("gz", "gy"),
        P("gz", "gy"),
        P(),
        P(("gz", "gy"), None, None),
        P(("gz", "gy"), None),
    )
    out_specs = (
        P("gz", "gy"),
        P("gz", "gy"),
        P("gz", "gy"),
        P("gz", "gy"),
        P(("gz", "gy"), None, None),
        P(("gz", "gy"), None),
    )
    return jax.shard_map(body, mesh=mesh, in_specs=in_specs, out_specs=out_specs, check_vma=False)
```

profile of v0, /device:TPU:1, one launch (start us, length us, event | category | flops | bytes accessed | tf_op | source)
XLA Modules:
  0.0 261.0 jit_solution(6800123248854732867)
XLA Ops:
  1.6 4.0 %collective-permute-start.3 = (f32[2,48,48]{2,1,0:T(8,128)S(1)}, f32[2,48,48]{2,1,0:T(8,128)S(1)}, u32[]{:S(2)}, u32[]{:S(2)}) collective-permute-start(f32[2,48,48]{2,1,0:T(8,128)S(1)} %get-tuple-element.32), channel_id=1, source_target_pairs={{0,1},{1,2},{2,3},{4,5},{5,6},{6,7},{8,9},{9,10},{10,11},{12,13},{... | collective-permute-start | bytes 55304 | tf_op jit(solution)/shard_map/ppermute | solution.py:36
  5.6 1.3 collective-permute-start.2
  7.8 4.0 %collective-permute-start.1 = (f32[2,1,1536]{2,1,0:T(1,128)S(1)}, f32[2,1,1536]{2,1,0:T(1,128)S(1)}, u32[]{:S(2)}, u32[]{:S(2)}) collective-permute-start(f32[2,1,1536]{2,1,0:T(1,128)S(1)} %get-tuple-element.30), channel_id=1, source_target_pairs={{0,4},{4,8},{8,12},{12,16},{16,20},{20,24},{24,28},{28,32},{32,36}... | collective-permute-start | bytes 36872 | tf_op jit(solution)/shard_map/ppermute | solution.py:36
  11.8 1.9 collective-permute-start
  15.6 4.1 %scatter_custom_fusion = f32[1792]{0:T(1024)S(1)} fusion(s32[576]{0:T(1024)S(1)} %fusion.37, f32[576]{0:T(1024)S(1)} %reshape.154, f32[]{:T(128)} %constant.35.clone.1), kind=kCustom, calls=%fused_computation.135 | custom fusion | bytes 7172 | tf_op jit(solution)/shard_map/scatter | solution.py:196
  20.4 11.7 %all-to-all-start = ((f32[128,14,1]{1,2,0:T(1,128)}), f32[128,14,1]{1,2,0:T(1,128)S(1)}, u32[]{:S(2)}, u32[]{:S(2)}) async-start(f32[128,14,1]{1,2,0:T(1,128)} %bitcast.27), calls=%async_computation | async-start | bytes 131072 | tf_op jit(solution)/shard_map/all_to_all | solution.py:201
  32.1 1.3 slice_maximum_fusion.2
  33.4 1.3 fusion.9
  35.2 4.1 %scatter_custom_fusion.1 = f32[1792]{0:T(1024)S(1)} fusion(s32[576]{0:T(1024)S(1)} %fusion.37, f32[576]{0:T(1024)S(1)} %reshape.162, f32[]{:T(128)} %constant.27.clone.1), kind=kCustom, calls=%fused_computation.133 | custom fusion | bytes 7172 | tf_op jit(solution)/shard_map/scatter | solution.py:198
  42.2 3.3 %collective-permute-start.7 = (f32[2,48,48]{2,1,0:T(8,128)S(1)}, f32[2,48,48]{2,1,0:T(8,128)S(1)}, u32[]{:S(2)}, u32[]{:S(2)}) collective-permute-start(f32[2,48,48]{2,1,0:T(8,128)S(1)} %get-tuple-element.28), channel_id=1, source_target_pairs={{0,1},{1,2},{2,3},{4,5},{5,6},{6,7},{8,9},{9,10},{10,11},{12,13},{... | collective-permute-start | bytes 55304 | tf_op jit(solution)/shard_map/ppermute | solution.py:36
  45.5 1.3 collective-permute-start.6
  46.8 3.6 %collective-permute-start.5 = (f32[2,1,1536]{2,1,0:T(1,128)S(1)}, f32[2,1,1536]{2,1,0:T(1,128)S(1)}, u32[]{:S(2)}, u32[]{:S(2)}) collective-permute-start(f32[2,1,1536]{2,1,0:T(1,128)S(1)} %get-tuple-element.26), channel_id=1, source_target_pairs={{0,4},{4,8},{8,12},{12,16},{16,20},{20,24},{24,28},{28,32},{32,36}... | collective-permute-start | bytes 36872 | tf_op jit(solution)/shard_map/ppermute | solution.py:36
  50.4 1.9 collective-permute-start.4
  52.4 3.0 %collective-permute-done.4 = f32[2,1,1536]{2,1,0:T(1,128)S(1)} collective-permute-done((f32[2,1,1536]{2,1,0:T(1,128)S(1)}, f32[2,1,1536]{2,1,0:T(1,128)S(1)}, u32[]{:S(2)}, u32[]{:S(2)}) %collective-permute-start.4) | collective-permute-done | bytes 12320 | tf_op jit(solution)/shard_map/ppermute | solution.py:38
  55.4 1.2 add_divide_fusion.3
  57.5 4.3 %collective-permute-start.11 = (f32[2,48,48]{2,1,0:T(8,128)S(1)}, f32[2,48,48]{2,1,0:T(8,128)S(1)}, u32[]{:S(2)}, u32[]{:S(2)}) collective-permute-start(f32[2,48,48]{2,1,0:T(8,128)S(1)} %get-tuple-element.24), channel_id=1, source_target_pairs={{0,1},{1,2},{2,3},{4,5},{5,6},{6,7},{8,9},{9,10},{10,11},{12,13},{... | collective-permute-start | bytes 55304 | tf_op jit(solution)/shard_map/ppermute | solution.py:36
  61.8 1.3 collective-permute-start.10
  63.1 2.2 collective-permute-start.9
  65.3 2.1 collective-permute-start.8
  67.5 2.8 %collective-permute-done.8 = f32[2,1,1536]{2,1,0:T(1,128)S(1)} collective-permute-done((f32[2,1,1536]{2,1,0:T(1,128)S(1)}, f32[2,1,1536]{2,1,0:T(1,128)S(1)}, u32[]{:S(2)}, u32[]{:S(2)}) %collective-permute-start.8) | collective-permute-done | bytes 12320 | tf_op jit(solution)/shard_map/ppermute | solution.py:38
  70.3 2.2 add_multiply_fusion
  72.7 14.4 %all-to-all-start.1 = ((f32[128,14,1]{1,2,0:T(1,128)}), f32[128,14,1]{1,2,0:T(1,128)S(1)}, u32[]{:S(2)}, u32[]{:S(2)}) async-start(f32[128,14,1]{1,2,0:T(1,128)} %bitcast.28), calls=%async_computation.1 | async-start | bytes 131072 | tf_op jit(solution)/shard_map/all_to_all | solution.py:202
  87.9 2.1 broadcast_in_dim.70
  89.9 58.0 %scatter_fusion = f32[1792,3,128]{2,1,0:T(4,128)} fusion(f32[1792,3,128]{2,1,0:T(4,128)} %broadcast_in_dim.70, s32[576]{0:T(1024)S(1)} %fusion.37, f32[576,3,128]{2,1,0:T(4,128)S(1)} %pad_maximum_fusion), kind=kCustom, calls=%fused_computation.3 | custom fusion | bytes 2656512 | tf_op jit(solution)/shard_map/scatter | solution.py:192
  147.9 10.2 %all-to-all-start.2 = ((f32[1792,3,128]{2,1,0:T(4,128)}), f32[1792,3,128]{2,1,0:T(4,128)}, u32[]{:S(2)}, u32[]{:S(2)}) async-start(f32[1792,3,128]{2,1,0:T(4,128)} %scatter_fusion), calls=%async_computation.2 | async-start | bytes 7340032 | tf_op jit(solution)/shard_map/all_to_all | solution.py:200
  160.4 45.0 %all-to-all-done.2 = f32[1792,3,128]{2,1,0:T(4,128)} async-done(((f32[1792,3,128]{2,1,0:T(4,128)}), f32[1792,3,128]{2,1,0:T(4,128)}, u32[]{:S(2)}, u32[]{:S(2)}) %all-to-all-start.2) | async-done | bytes 2752544 | tf_op jit(solution)/shard_map/all_to_all | solution.py:200
  205.4 7.2 %fusion.41 = (f32[1792,1,128]{2,1,0:T(1,128)S(1)}, f32[1792,1,128]{2,1,0:T(1,128)S(1)}, f32[1792,1,128]{2,1,0:T(1,128)S(1)}) fusion(f32[1792,3,128]{2,1,0:T(4,128)} %all-to-all-done.2), kind=kLoop, calls=%fused_computation.141 | loop fusion | bytes 5505024 | tf_op jit(solution)/shard_map/slice | solution.py:206
  213.0 19.4 %fusion = (f32[1792,8,128]{2,1,0:T(8,128)}, f32[1792,128]{1,0:T(8,128)S(1)}) fusion(f32[1792,8,128]{2,1,0:T(8,128)} %param.14, f32[1792,128]{1,0:T(8,128)S(1)} %broadcast_multiply_fusion, f32[8]{0:T(128)S(1)} %power_multiply_fusion, f32[1792,128]{1,0:T(8,128)S(1)} %fusion.4, pred[1792,128]{1,0:T(8,128)(4,1)S(1)} %broadcast_compare_fusion), kind=kLoop, calls=%fused_computation.7 | loop fusion | flops 14450688 | bytes 17661984 | tf_op jit(solution)/shard_map/jit(_where)/select_n | solution.py:118
  232.4 1.9 compare_select_fusion
  235.4 3.7 %all-to-all-start.3 = ((f32[128,14,128]{2,1,0:T(8,128)}), f32[128,14,128]{2,1,0:T(8,128)S(1)}, u32[]{:S(2)}, u32[]{:S(2)}) async-start(f32[128,14,128]{2,1,0:T(8,128)} %all_to_all.28), calls=%async_computation.3 | async-start | bytes 2097152 | tf_op jit(solution)/shard_map/all_to_all | solution.py:213
  239.1 19.4 %all-to-all-done.3 = f32[128,14,128]{2,1,0:T(8,128)S(1)} async-done(((f32[128,14,128]{2,1,0:T(8,128)}), f32[128,14,128]{2,1,0:T(8,128)S(1)}, u32[]{:S(2)}, u32[]{:S(2)}) %all-to-all-start.3) | async-done | bytes 917536 | tf_op jit(solution)/shard_map/all_to_all | solution.py:213
  258.6 1.6 gather_fusion
  (75 shorter events, 14.1 us)
Async XLA Ops:
  0.6 39.4 %copy-start.1 = (f32[48,1536]{1,0:T(8,128)S(1)}, f32[48,1536]{1,0:T(8,128)}, u32[]{:S(2)}) copy-start(f32[48,1536]{1,0:T(8,128)} %param.9) | copy-start | bytes 884740
  0.6 39.4 %copy-start = (f32[48,1536]{1,0:T(8,128)S(1)}, f32[48,1536]{1,0:T(8,128)}, u32[]{:S(2)}) copy-start(f32[48,1536]{1,0:T(8,128)} %param.8) | copy-start | bytes 884740
  0.7 34.1 %copy-start.6 = (s32[192]{0:T(256)S(1)}, s32[192]{0:T(256)}, u32[]{:S(2)}) copy-start(s32[192]{0:T(256)} %param.13) | copy-start | bytes 2308
  0.7 39.4 %copy-start.2 = (f32[48,1536]{1,0:T(8,128)S(1)}, f32[48,1536]{1,0:T(8,128)}, u32[]{:S(2)}) copy-start(f32[48,1536]{1,0:T(8,128)} %param.10) | copy-start | bytes 884740
  1.6 38.4 %collective-permute-start.3 = (f32[2,48,48]{2,1,0:T(8,128)S(1)}, f32[2,48,48]{2,1,0:T(8,128)S(1)}, u32[]{:S(2)}, u32[]{:S(2)}) collective-permute-start(f32[2,48,48]{2,1,0:T(8,128)S(1)} %get-tuple-element.32), channel_id=1, source_target_pairs={{0,1},{1,2},{2,3},{4,5},{5,6},{6,7},{8,9},{9,10},{10,11},{12,13},{... | collective-permute-start | bytes 55304 | tf_op jit(solution)/shard_map/ppermute | solution.py:36
  5.6 34.4 %collective-permute-start.2 = (f32[2,48,48]{2,1,0:T(8,128)S(1)}, f32[2,48,48]{2,1,0:T(8,128)S(1)}, u32[]{:S(2)}, u32[]{:S(2)}) collective-permute-start(f32[2,48,48]{2,1,0:T(8,128)S(1)} %get-tuple-element.31), channel_id=1, source_target_pairs={{1,0},{2,1},{3,2},{5,4},{6,5},{7,6},{9,8},{10,9},{11,10},{13,12},{... | collective-permute-start | bytes 55304 | tf_op jit(solution)/shard_map/ppermute | solution.py:38
  7.8 32.2 %collective-permute-start.1 = (f32[2,1,1536]{2,1,0:T(1,128)S(1)}, f32[2,1,1536]{2,1,0:T(1,128)S(1)}, u32[]{:S(2)}, u32[]{:S(2)}) collective-permute-start(f32[2,1,1536]{2,1,0:T(1,128)S(1)} %get-tuple-element.30), channel_id=1, source_target_pairs={{0,4},{4,8},{8,12},{12,16},{16,20},{20,24},{24,28},{28,32},{32,36}... | collective-permute-start | bytes 36872 | tf_op jit(solution)/shard_map/ppermute | solution.py:36
  11.8 28.2 %collective-permute-start = (f32[2,1,1536]{2,1,0:T(1,128)S(1)}, f32[2,1,1536]{2,1,0:T(1,128)S(1)}, u32[]{:S(2)}, u32[]{:S(2)}) collective-permute-start(f32[2,1,1536]{2,1,0:T(1,128)S(1)} %get-tuple-element.29), channel_id=1, source_target_pairs={{4,0},{8,4},{12,8},{16,12},{20,16},{24,20},{28,24},{32,28},{36,32}... | collective-permute-start | bytes 36872 | tf_op jit(solution)/shard_map/ppermute | solution.py:38
  20.4 52.3 %all-to-all-start = ((f32[128,14,1]{1,2,0:T(1,128)}), f32[128,14,1]{1,2,0:T(1,128)S(1)}, u32[]{:S(2)}, u32[]{:S(2)}) async-start(f32[128,14,1]{1,2,0:T(1,128)} %bitcast.27), calls=%async_computation | async-start | bytes 131072 | tf_op jit(solution)/shard_map/all_to_all | solution.py:201
  42.2 13.2 %collective-permute-start.7 = (f32[2,48,48]{2,1,0:T(8,128)S(1)}, f32[2,48,48]{2,1,0:T(8,128)S(1)}, u32[]{:S(2)}, u32[]{:S(2)}) collective-permute-start(f32[2,48,48]{2,1,0:T(8,128)S(1)} %get-tuple-element.28), channel_id=1, source_target_pairs={{0,1},{1,2},{2,3},{4,5},{5,6},{6,7},{8,9},{9,10},{10,11},{12,13},{... | collective-permute-start | bytes 55304 | tf_op jit(solution)/shard_map/ppermute | solution.py:36
  45.5 9.9 %collective-permute-start.6 = (f32[2,48,48]{2,1,0:T(8,128)S(1)}, f32[2,48,48]{2,1,0:T(8,128)S(1)}, u32[]{:S(2)}, u32[]{:S(2)}) collective-permute-start(f32[2,48,48]{2,1,0:T(8,128)S(1)} %get-tuple-element.27), channel_id=1, source_target_pairs={{1,0},{2,1},{3,2},{5,4},{6,5},{7,6},{9,8},{10,9},{11,10},{13,12},{... | collective-permute-start | bytes 55304 | tf_op jit(solution)/shard_map/ppermute | solution.py:38
  46.8 5.6 %collective-permute-start.5 = (f32[2,1,1536]{2,1,0:T(1,128)S(1)}, f32[2,1,1536]{2,1,0:T(1,128)S(1)}, u32[]{:S(2)}, u32[]{:S(2)}) collective-permute-start(f32[2,1,1536]{2,1,0:T(1,128)S(1)} %get-tuple-element.26), channel_id=1, source_target_pairs={{0,4},{4,8},{8,12},{12,16},{16,20},{20,24},{24,28},{28,32},{32,36}... | collective-permute-start | bytes 36872 | tf_op jit(solution)/shard_map/ppermute | solution.py:36
  50.4 5.0 %collective-permute-start.4 = (f32[2,1,1536]{2,1,0:T(1,128)S(1)}, f32[2,1,1536]{2,1,0:T(1,128)S(1)}, u32[]{:S(2)}, u32[]{:S(2)}) collective-permute-start(f32[2,1,1536]{2,1,0:T(1,128)S(1)} %get-tuple-element.25), channel_id=1, source_target_pairs={{4,0},{8,4},{12,8},{16,12},{20,16},{24,20},{28,24},{32,28},{36,32}... | collective-permute-start | bytes 36872 | tf_op jit(solution)/shard_map/ppermute | solution.py:38
  57.5 12.8 %collective-permute-start.11 = (f32[2,48,48]{2,1,0:T(8,128)S(1)}, f32[2,48,48]{2,1,0:T(8,128)S(1)}, u32[]{:S(2)}, u32[]{:S(2)}) collective-permute-start(f32[2,48,48]{2,1,0:T(8,128)S(1)} %get-tuple-element.24), channel_id=1, source_target_pairs={{0,1},{1,2},{2,3},{4,5},{5,6},{6,7},{8,9},{9,10},{10,11},{12,13},{... | collective-permute-start | bytes 55304 | tf_op jit(solution)/shard_map/ppermute | solution.py:36
  61.8 8.5 %collective-permute-start.10 = (f32[2,48,48]{2,1,0:T(8,128)S(1)}, f32[2,48,48]{2,1,0:T(8,128)S(1)}, u32[]{:S(2)}, u32[]{:S(2)}) collective-permute-start(f32[2,48,48]{2,1,0:T(8,128)S(1)} %get-tuple-element.23), channel_id=1, source_target_pairs={{1,0},{2,1},{3,2},{5,4},{6,5},{7,6},{9,8},{10,9},{11,10},{13,12},{... | collective-permute-start | bytes 55304 | tf_op jit(solution)/shard_map/ppermute | solution.py:38
  63.1 4.4 %collective-permute-start.9 = (f32[2,1,1536]{2,1,0:T(1,128)S(1)}, f32[2,1,1536]{2,1,0:T(1,128)S(1)}, u32[]{:S(2)}, u32[]{:S(2)}) collective-permute-start(f32[2,1,1536]{2,1,0:T(1,128)S(1)} %get-tuple-element.22), channel_id=1, source_target_pairs={{0,4},{4,8},{8,12},{12,16},{16,20},{20,24},{24,28},{28,32},{32,36}... | collective-permute-start | bytes 36872 | tf_op jit(solution)/shard_map/ppermute | solution.py:36
  65.3 5.0 %collective-permute-start.8 = (f32[2,1,1536]{2,1,0:T(1,128)S(1)}, f32[2,1,1536]{2,1,0:T(1,128)S(1)}, u32[]{:S(2)}, u32[]{:S(2)}) collective-permute-start(f32[2,1,1536]{2,1,0:T(1,128)S(1)} %get-tuple-element.21), channel_id=1, source_target_pairs={{4,0},{8,4},{12,8},{16,12},{20,16},{24,20},{28,24},{32,28},{36,32}... | collective-permute-start | bytes 36872 | tf_op jit(solution)/shard_map/ppermute | solution.py:38
  72.6 17.4 %copy-start.3 = (f32[48,1536]{1,0:T(8,128)}, f32[48,1536]{1,0:T(8,128)S(1)}, u32[]{:S(2)}) copy-start(f32[48,1536]{1,0:T(8,128)S(1)} %get-tuple-element.8) | copy-start | bytes 884740
  72.6 17.3 %copy-start.4 = (f32[48,1536]{1,0:T(8,128)}, f32[48,1536]{1,0:T(8,128)S(1)}, u32[]{:S(2)}) copy-start(f32[48,1536]{1,0:T(8,128)S(1)} %broadcast_multiply_fusion.1) | copy-start | bytes 884740
  72.7 75.2 %all-to-all-start.1 = ((f32[128,14,1]{1,2,0:T(1,128)}), f32[128,14,1]{1,2,0:T(1,128)S(1)}, u32[]{:S(2)}, u32[]{:S(2)}) async-start(f32[128,14,1]{1,2,0:T(1,128)} %bitcast.28), calls=%async_computation.1 | async-start | bytes 131072 | tf_op jit(solution)/shard_map/all_to_all | solution.py:202
  147.9 57.5 %all-to-all-start.2 = ((f32[1792,3,128]{2,1,0:T(4,128)}), f32[1792,3,128]{2,1,0:T(4,128)}, u32[]{:S(2)}, u32[]{:S(2)}) async-start(f32[1792,3,128]{2,1,0:T(4,128)} %scatter_fusion), calls=%async_computation.2 | async-start | bytes 7340032 | tf_op jit(solution)/shard_map/all_to_all | solution.py:200
  212.9 19.4 %copy-start.5 = (f32[1792,128]{1,0:T(8,128)S(1)}, f32[1792,128]{1,0:T(8,128)}, u32[]{:S(2)}) copy-start(f32[1792,128]{1,0:T(8,128)} %param.15) | copy-start | bytes 2752516
  235.4 23.1 %all-to-all-start.3 = ((f32[128,14,128]{2,1,0:T(8,128)}), f32[128,14,128]{2,1,0:T(8,128)S(1)}, u32[]{:S(2)}, u32[]{:S(2)}) async-start(f32[128,14,128]{2,1,0:T(8,128)} %all_to_all.28), calls=%async_computation.3 | async-start | bytes 2097152 | tf_op jit(solution)/shard_map/all_to_all | solution.py:213
where the time goes:
time: 263 us; the launch traced here: 261 us
  local copies, waits for them, and re-layouts  82.8 us (31%)
  starting transfers between devices  71.1 us (27%)
  waiting for transfers between devices  70.3 us (27%)
  other arithmetic  35.6 us (14%)
    scatter x1, local copies, waits for them, and re-layouts, body(): jnp.zeros((total_slots, 3, PARCEL_SITES), jnp.float32).at[flat_slot]  58 us
    all_to_all x1, waiting for transfers between devices, body(): lax.all_to_all(send_fields, ('gz', 'gy'), split_axis=0, concat_axis=0, ti...  45 us
    ppermute x6, starting transfers between devices, with_halo(): lax.ppermute(tail, axis, [(i, (i + 1) % count) for i in range(ends)])  21.4 us
    all_to_all x1, waiting for transfers between devices, body(): lax.all_to_all(small_change, ('gz', 'gy'), split_axis=0, concat_axis=0, t...  19.4 us
    select_n x1, other arithmetic, viscous_strain_advance(): series_result = jnp.where(placed[..., None, :], chain_new, series_prior)  19.4 us
    all_to_all x1, starting transfers between devices, body(): lax.all_to_all(send_age, ('gz', 'gy'), split_axis=0, concat_axis=0, tiled...  14.4 us
    all_to_all x1, starting transfers between devices, body(): lax.all_to_all(send_count, ('gz', 'gy'), split_axis=0, concat_axis=0, til...  11.7 us
    all_to_all x1, starting transfers between devices, body(): lax.all_to_all(send_fields, ('gz', 'gy'), split_axis=0, concat_axis=0, ti...  10.2 us
  transfers between devices with their start and end apart: 16, of which 4 were waited for; matrix products, arithmetic and copies ran while one was open for 32% of the time, Pallas kernels for 0%

commit v1 on v0

v1 whole, which is shorter than its diff:
```python
import functools
import math

import jax
import jax.numpy as jnp
from jax import lax
from jax.experimental import pallas as pl
from jax.experimental.pallas import tpu as pltpu
from jax.sharding import PartitionSpec as P

NX = 48
LANES = 128
LIFT = 8
CAP = 14
UNITS = 8
ROWS = 48
TILES = 12
COLS = TILES * LANES
WIDE = (TILES + 3) * LANES
OWN = 2 * LANES
SEND = 32
BACK = 16
AGE_ROW = 14

D0 = 0.05 + 0.95 / (1.0 + 5.0**16)

F32 = jnp.float32
VM = pltpu.VMEM
SM = pltpu.SMEM


def rate_of(u, h, a):
    q = 7.5 - 7.5 * h
    q = q * q
    return 0.05 * (1.0 - a) * jnp.exp(0.5 * u) / (1.0 + q * q)


def excess_diffusivity(h):
    p = 5.0 * (1.0 - h)
    p = p * p
    p = p * p
    p = p * p
    p = p * p
    return (0.05 - D0) + 0.95 / (1.0 + p)


def lanes_of(shape):
    return lax.broadcasted_iota(jnp.int32, shape, len(shape) - 1)


def split_position(p):
    owner = lax.shift_right_logical(p * 37450, 19)
    return owner, p - CAP * owner


def pack_y_kernel(ul, ur, hl, hr, al, ar, to_left, to_right):
    lane = lanes_of((ROWS, LANES))
    first, second = slice(0, LANES), slice(LANES, 2 * LANES)
    to_left[0:ROWS, :] = ul[:, first]
    to_left[ROWS : 2 * ROWS, :] = hl[:, first]
    far_u = pltpu.roll(ul[:, second], 96, 1)
    far_h = pltpu.roll(hl[:, second], 112, 1)
    to_left[2 * ROWS : 3 * ROWS, :] = jnp.where(
        lane < 96, al[:, first], jnp.where(lane < 112, far_u, far_h)
    )
    to_right[0:ROWS, :] = ur[:, second]
    to_right[ROWS : 2 * ROWS, :] = hr[:, second]
    far_u = pltpu.roll(ur[:, first], 16, 1)
    far_h = pltpu.roll(hr[:, first], 32, 1)
    to_right[2 * ROWS : 3 * ROWS, :] = jnp.where(
        lane >= 32, ar[:, second], jnp.where(lane < 16, far_u, far_h)
    )


def pack_y(u, h, a):
    left = pl.BlockSpec((ROWS, 2 * LANES), lambda i: (0, 0))
    right = pl.BlockSpec((ROWS, 2 * LANES), lambda i: (0, COLS // (2 * LANES) - 1))
    whole = pl.BlockSpec((3 * ROWS, LANES), lambda i: (0, 0))
    shape = jax.ShapeDtypeStruct((3 * ROWS, LANES), F32)
    return pl.pallas_call(
        pack_y_kernel,
        grid=(1,),
        out_shape=(shape, shape),
        in_specs=[left, right, left, right, left, right],
        out_specs=(whole, whole),
    )(u, u, h, h, a, a)


def side_tiles(from_left, from_right, lo, n):
    lane = lanes_of((n, LANES))
    rows = [slice(f * ROWS + lo, f * ROWS + lo + n) for f in range(3)]
    lx, rx = from_left[rows[2], :], from_right[rows[2], :]
    zero = jnp.zeros((n, LANES), F32)

    def far(left_shift, right_shift):
        return jnp.where(
            lane < 16,
            pltpu.roll(rx, right_shift, 1),
            jnp.where(lane >= 112, pltpu.roll(lx, left_shift, 1), zero),
        )

    return (
        (far(112, 32), from_left[rows[0], :], from_right[rows[0], :]),
        (far(96, 16), from_left[rows[1], :], from_right[rows[1], :]),
        (zero, jnp.where(lane >= 32, lx, zero), jnp.where(lane < 96, rx, zero)),
    )


def pack_z_kernel(u0, u1, h0, h1, a0, a1, from_left, from_right, up, down):
    row = lax.broadcasted_iota(jnp.int32, (8, WIDE), 0)
    for out, (u, h, a), lo, shifts in (
        (up, (u0, h0, a0), 0, (0, 3, 6)),
        (down, (u1, h1, a1), ROWS - 8, (3, 6, 0)),
    ):
        sides = side_tiles(from_left, from_right, lo, 8)
        wide = []
        for field, side, shift in zip((u, h, a), sides, shifts):
            v = jnp.concatenate([side[0], side[1], field[...], side[2]], axis=1)
            wide.append(pltpu.roll(v, shift, 0) if shift else v)
        out[...] = jnp.where(row < 3, wide[0], jnp.where(row < 6, wide[1], wide[2]))


def pack_z(u, h, a, from_left, from_right):
    top = pl.BlockSpec((8, COLS), lambda i: (0, 0))
    bottom = pl.BlockSpec((8, COLS), lambda i: (ROWS // 8 - 1, 0))
    side = pl.BlockSpec((3 * ROWS, LANES), lambda i: (0, 0))
    out = pl.BlockSpec((8, WIDE), lambda i: (0, 0))
    shape = jax.ShapeDtypeStruct((8, WIDE), F32)
    return pl.pallas_call(
        pack_z_kernel,
        grid=(1,),
        out_shape=(shape, shape),
        in_specs=[top, bottom, top, bottom, top, bottom, side, side],
        out_specs=(out, out),
    )(u, u, h, h, a, a, from_left, from_right)


def table_kernel(place, times, keeper, table):
    lane = lanes_of((ROWS, LANES))
    solid = []
    for r in range(ROWS // LIFT):
        age = 2400.0 - jnp.full((LIFT, LANES), times[place[0] * (ROWS // LIFT) + r], jnp.int32).astype(F32)
        solid.append(jnp.sqrt(600.0 / age) + 0.2)
    solid = jnp.concatenate(solid, axis=0)
    owners, slots = [], []
    for j in range(TILES):
        owner, slot = split_position(jnp.broadcast_to(keeper[:, j : j + 1], (ROWS, LANES)))
        owners.append(jnp.where(owner == lane, 1.0, 0.0))
        slots.append(jnp.where(slot == lane, solid, 0.0))
    table[...] = lax.dot_general(
        jnp.concatenate(owners, axis=0),
        jnp.concatenate(slots, axis=0),
        (((0,), (0,)), ((), ())),
        precision=lax.Precision.HIGHEST,
        preferred_element_type=F32,
    )


def solid_table(place, times, keeper):
    return pl.pallas_call(
        table_kernel,
        out_shape=jax.ShapeDtypeStruct((LANES, LANES), F32),
        in_specs=[
            pl.BlockSpec(memory_space=SM),
            pl.BlockSpec(memory_space=SM),
            pl.BlockSpec(memory_space=VM),
        ],
        out_specs=pl.BlockSpec(memory_space=VM),
    )(place, times, keeper)


def sweep_kernel(
    place,
    keeper,
    tally,
    u_in,
    h_in,
    a_in,
    from_left,
    from_right,
    above,
    below,
    table,
    t_out,
    h_out,
    m_out,
    send,
    u_first,
    h_first,
    a_wide,
    fields,
    phi_buf,
    stress_buf,
):
    gz, gy, last_z, last_y = place[0], place[1], place[2], place[3]
    tiles = ROWS // 8 + 1

    send[...] = jnp.zeros_like(send)

    sides = side_tiles(from_left, from_right, 0, ROWS)
    for wide, own, side in zip((u_first, h_first, a_wide), (u_in, h_in, a_in), sides):
        wide[0:ROWS, 0:LANES] = side[0]
        wide[0:ROWS, LANES:OWN] = side[1]
        wide[0:ROWS, OWN : OWN + COLS] = own[...]
        wide[0:ROWS, OWN + COLS : WIDE] = side[2]
    row8 = lax.broadcasted_iota(jnp.int32, (8, WIDE), 0)
    zero = jnp.zeros((8, WIDE), F32)
    top, bottom = above[...], below[...]
    for wide, down_shift, up_shift in ((u_first, 0, 5), (h_first, 5, 2), (a_wide, 2, 0)):
        b = pltpu.roll(bottom, down_shift, 0) if down_shift else bottom
        t = pltpu.roll(top, up_shift, 0) if up_shift else top
        wide[ROWS : ROWS + 8, :] = jnp.where(row8 < 3, b, jnp.where(row8 >= 5, t, zero))

    column = lanes_of((8, WIDE))
    line = lax.rem(column + (16 * NX - OWN), NX)
    not_first, not_last = line != 0, line != NX - 1
    on_left = (column >= 64) & (column < OWN)
    on_own = (column >= OWN) & (column < OWN + COLS)
    left_is, right_is = (gy > 0).astype(jnp.int32), (gy < last_y).astype(jnp.int32)
    above_is, below_is = (gz > 0).astype(jnp.int32), (gz < last_z).astype(jnp.int32)
    inside_columns = jnp.where(on_own, 1, jnp.where(on_left, left_is, right_is))

    def derived(h):
        d = excess_diffusivity(h)
        return d, d * h

    def fill(r, carry):
        rows = pl.ds(pl.multiple_of(r * 8, 8), 8)
        h = h_first[rows, :]
        d, dh = derived(h)
        fields[0, 0, rows, :] = u_first[rows, :]
        fields[0, 1, rows, :] = h
        fields[0, 2, rows, :] = d
        fields[0, 3, rows, :] = dh
        return carry

    lax.fori_loop(0, tiles, fill, 0)

    def step(src, r):
        here = pl.ds(pl.multiple_of(r * 8, 8), 8)
        before = pl.ds(pl.multiple_of(jnp.where(r == 0, tiles - 1, r - 1) * 8, 8), 8)
        after = pl.ds(pl.multiple_of(jnp.where(r == tiles - 1, 0, r + 1) * 8, 8), 8)

        def around(f):
            v = fields[src, f, here, :]
            lower, upper = fields[src, f, before, :], fields[src, f, after, :]
            total = pltpu.roll(jnp.where(row8 == 0, upper, v), 7, 0)
            total = total + pltpu.roll(jnp.where(row8 == 7, lower, v), 1, 0)
            total = total + pltpu.roll(v, WIDE - NX, 1)
            total = total + pltpu.roll(v, NX, 1)
            total = total + pltpu.roll(jnp.where(not_first, v, 0.0), WIDE - 1, 1)
            total = total + pltpu.roll(jnp.where(not_last, v, 0.0), 1, 1)
            return total

        u, h, d = fields[src, 0, here, :], fields[src, 1, here, :], fields[src, 2, here, :]
        r_now = rate_of(u, h, a_wide[here, :])
        u_next = (u_first[here, :] + 4.0 * r_now + around(0)) * (1.0 / 7.0)
        conduct = 3.0 * (d + 2.0 * D0) + 0.5 * around(2)
        inflow = 0.5 * ((d + 2.0 * D0) * around(1) + around(3))
        h_next = (h_first[here, :] - 0.5 * r_now + inflow) / (1.0 + conduct)
        return u_next, h_next

    def middle(src):
        def run(r, carry):
            rows = pl.ds(pl.multiple_of(r * 8, 8), 8)
            u, h = step(src, r)
            own_rows = (r < tiles - 1).astype(jnp.int32)
            below_in, above_in = jnp.maximum(own_rows, below_is), jnp.maximum(own_rows, above_is)
            keep = inside_columns * jnp.where(row8 < 4, below_in, above_in) > 0
            u, h = jnp.where(keep, u, 0.0), jnp.where(keep, h, 0.0)
            d, dh = derived(h)
            fields[1 - src, 0, rows, :] = u
            fields[1 - src, 1, rows, :] = h
            fields[1 - src, 2, rows, :] = d
            fields[1 - src, 3, rows, :] = dh
            return carry

        lax.fori_loop(0, tiles, run, 0)

    middle(0)
    middle(1)

    lane8 = lanes_of((8, LANES))

    def last(r, carry):
        rows = pl.ds(pl.multiple_of(r * 8, 8), 8)
        u, h = step(0, r)
        u, h = u[:, OWN : OWN + COLS], h[:, OWN : OWN + COLS]
        a = a_in[rows, :]
        m = a + rate_of(u, h, a)
        t_out[rows, :] = u
        h_out[rows, :] = h
        m_out[rows, :] = m
        stress = -m * (0.5 * u + 2.0 * (1.0 - h))
        phi = jnp.exp(0.3 * u) * (0.1 + 0.9 * h * h)
        counts = tally[rows, :]
        for j in range(TILES):
            part = slice(j * LANES, (j + 1) * LANES)
            placed = lane8 < jnp.broadcast_to(counts[:, j : j + 1], (8, LANES))
            block_rows = pl.ds(pl.multiple_of(j * ROWS + r * 8, 8), 8)
            phi_buf[block_rows, :] = jnp.where(placed, phi[:, part], 0.0)
            stress_buf[block_rows, :] = stress[:, part]
        return carry

    lax.fori_loop(0, tiles - 1, last, 0)

    for o in range(LANES):
        send[o * SEND + AGE_ROW : o * SEND + AGE_ROW + 1, :] = table[o : o + 1, :]

    def scatter(z, carry):
        for j in range(TILES):
            owner, slot = split_position(keeper[z, j])
            at = owner * SEND + slot
            block = pl.ds(j * ROWS + z, 1)
            send[pl.ds(at, 1), :] = phi_buf[block, :]
            send[pl.ds(at + 16, 1), :] = stress_buf[block, :]
        return carry

    lax.fori_loop(0, ROWS, scatter, 0)


def sweeps(place, keeper, tally, u, h, a, from_left, from_right, above, below, table):
    grid_shape = jax.ShapeDtypeStruct((ROWS, COLS), F32)
    wide = pltpu.VMEM((ROWS + 8, WIDE), F32)
    return pl.pallas_call(
        sweep_kernel,
        out_shape=(grid_shape, grid_shape, grid_shape, jax.ShapeDtypeStruct((LANES * SEND, LANES), F32)),
        in_specs=[pl.BlockSpec(memory_space=SM)] * 2 + [pl.BlockSpec(memory_space=VM)] * 9,
        out_specs=[pl.BlockSpec(memory_space=VM)] * 4,
        scratch_shapes=[
            wide,
            wide,
            wide,
            pltpu.VMEM((2, 4, ROWS + 8, WIDE), F32),
            pltpu.VMEM((TILES * ROWS, LANES), F32),
            pltpu.VMEM((TILES * ROWS, LANES), F32),
        ],
        compiler_params=pltpu.CompilerParams(vmem_limit_bytes=32 * 2**20),
    )(place, keeper, tally, u, h, a, from_left, from_right, above, below, table)


GROUP = 8


def decay_rates():
    unit = lax.broadcasted_iota(jnp.int32, (UNITS, LANES), 0)
    scale = jnp.zeros((UNITS, LANES), F32)
    for m in range(UNITS):
        scale = jnp.where(unit == m, -1.0 / (0.1 * 3.0**m), scale)
    return scale


def unit_change(chain, phi, stress, k, scale):
    row = slice(k, k + 1)
    b = jnp.exp(jnp.broadcast_to(phi[row, :], (UNITS, LANES)) * scale)
    return (1.0 - b) * (jnp.broadcast_to(stress[row, :], (UNITS, LANES)) - chain)


def sum_units(parts):
    row = lax.broadcasted_iota(jnp.int32, (8, LANES), 0)
    low = row < 4
    pairs = []
    for k in range(4):
        x, y = parts[k], parts[k + 4]
        pairs.append(jnp.where(low, x, y) + pltpu.roll(jnp.where(low, y, x), 4, 0))
    for step in (2, 1):
        first = (row & step) == 0
        pairs = [
            jnp.where(
                first,
                pairs[k] + pltpu.roll(pairs[k], 8 - step, 0),
                pairs[k + step] + pltpu.roll(pairs[k + step], step, 0),
            )
            for k in range(step)
        ]
    return pairs[0]


def creep_kernel(got, chain, tension, creep):
    scale = decay_rates()
    diagonal = lanes_of((BACK, LANES)) == lax.broadcasted_iota(jnp.int32, (BACK, LANES), 0)

    def one(s, carry):
        base = pl.multiple_of(s * SEND, SEND)
        phi, stress = got[pl.ds(base, 16), :], got[pl.ds(base + 16, 16), :]
        ages = jnp.broadcast_to(phi[AGE_ROW : AGE_ROW + 1, :], (BACK, LANES))
        solid = jnp.sum(jnp.where(diagonal, ages, 0.0), axis=1, keepdims=True)
        load = 0.15 * stress
        zero = jnp.zeros((UNITS, LANES), F32)
        changes = [unit_change(chain[s * CAP + k], phi, load, k, scale) for k in range(CAP)]
        changes += [zero] * (BACK - CAP)
        total = jnp.concatenate([sum_units(changes[:8]), sum_units(changes[8:])], axis=0)
        rows = pl.ds(pl.multiple_of(s * BACK, BACK), BACK)
        before = tension[rows, :]
        after = before / (1.0 + 0.2 * phi * before)
        creep[rows, :] = solid * total + 0.1 * phi * after * stress
        return carry

    lax.fori_loop(0, GROUP, one, 0)


def state_kernel(got, chain, tension, chain_out, tension_out):
    scale = decay_rates()

    def one(s, carry):
        base = pl.multiple_of(s * SEND, SEND)
        phi, stress = got[pl.ds(base, 16), :], got[pl.ds(base + 16, 16), :]
        load = 0.15 * stress
        for k in range(CAP):
            prior = chain[s * CAP + k]
            chain_out[s * CAP + k] = prior + unit_change(prior, phi, load, k, scale)
        rows = pl.ds(pl.multiple_of(s * BACK, BACK), BACK)
        before = tension[rows, :]
        tension_out[rows, :] = before / (1.0 + 0.2 * phi * before)
        return carry

    lax.fori_loop(0, GROUP, one, 0)


def owner_specs():
    return (
        pl.BlockSpec((GROUP * SEND, LANES), lambda i: (i, 0)),
        pl.BlockSpec((GROUP * CAP, UNITS, LANES), lambda i: (i, 0, 0)),
        pl.BlockSpec((GROUP * BACK, LANES), lambda i: (i, 0)),
    )


def creep_of(got, chain, tension):
    message, states, rows = owner_specs()
    return pl.pallas_call(
        creep_kernel,
        grid=(LANES // GROUP,),
        out_shape=jax.ShapeDtypeStruct((LANES * BACK, LANES), F32),
        in_specs=[message, states, rows],
        out_specs=rows,
        cost_estimate=pl.CostEstimate(flops=20 * chain.size, bytes_accessed=4 * chain.size, transcendentals=chain.size),
    )(got, chain, tension)


def states_of(got, chain, tension):
    message, states, rows = owner_specs()
    return pl.pallas_call(
        state_kernel,
        grid=(LANES // GROUP,),
        out_shape=(
            jax.ShapeDtypeStruct(chain.shape, F32),
            jax.ShapeDtypeStruct((LANES * BACK, LANES), F32),
        ),
        in_specs=[message, states, rows],
        out_specs=(states, rows),
        cost_estimate=pl.CostEstimate(flops=20 * chain.size, bytes_accessed=8 * chain.size, transcendentals=chain.size),
    )(got, chain, tension)


def collect_kernel(keeper, back, out, blocks):
    def line(z, carry):
        for j in range(TILES):
            owner, slot = split_position(keeper[z, j])
            blocks[pl.ds(j * ROWS + z, 1), :] = back[pl.ds(owner * BACK + slot, 1), :]
        return carry

    lax.fori_loop(0, ROWS, line, 0)
    for j in range(TILES):
        out[:, j * LANES : (j + 1) * LANES] = blocks[j * ROWS : (j + 1) * ROWS, :]


def collect(keeper, back):
    return pl.pallas_call(
        collect_kernel,
        out_shape=jax.ShapeDtypeStruct((ROWS, COLS), F32),
        in_specs=[pl.BlockSpec(memory_space=SM), pl.BlockSpec(memory_space=VM)],
        out_specs=pl.BlockSpec(memory_space=VM),
        scratch_shapes=[pltpu.VMEM((TILES * ROWS, LANES), F32)],
    )(keeper, back)


def both_ways(axis, to_lower, to_higher):
    ends = lax.axis_size(axis) - 1
    from_lower = lax.ppermute(to_higher, axis, [(i, i + 1) for i in range(ends)])
    from_higher = lax.ppermute(to_lower, axis, [(i + 1, i) for i in range(ends)])
    return from_lower, from_higher


def exchange(x):
    return lax.all_to_all(x, ("gz", "gy"), split_axis=0, concat_axis=0, tiled=True)


def body(u, h, a, tally, keeper, times, chain, tension):
    ends = [jnp.int32(lax.axis_size(n) - 1) for n in ("gz", "gy")]
    place = jnp.stack([lax.axis_index("gz"), lax.axis_index("gy"), *ends]).astype(jnp.int32)
    to_left, to_right = pack_y(u, h, a)
    from_left, from_right = both_ways("gy", to_left, to_right)
    table = solid_table(place, times, keeper)
    up, down = pack_z(u, h, a, from_left, from_right)
    above, below = both_ways("gz", up, down)
    t_new, h_new, m_new, send = sweeps(place, keeper, tally, u, h, a, from_left, from_right, above, below, table)
    got = exchange(send)
    tension_wide = jnp.pad(tension.reshape(LANES, CAP, LANES), ((0, 0), (0, BACK - CAP), (0, 0))).reshape(-1, LANES)
    creep = creep_of(got, chain, tension_wide)
    back = exchange(creep)
    chain_new, tension_new = states_of(got, chain, tension_wide)
    tension_new = tension_new.reshape(LANES, BACK, LANES)[:, :CAP].reshape(-1, LANES)
    return t_new, h_new, m_new, collect(keeper, back), chain_new, tension_new


def solution(mesh):
    grid = P("gz", "gy")
    owners = ("gz", "gy")
    return jax.shard_map(
        body,
        mesh=mesh,
        in_specs=(grid, grid, grid, grid, grid, P(), P(owners, None, None), P(owners, None)),
        out_specs=(grid, grid, grid, grid, P(owners, None, None), P(owners, None)),
        check_vma=False,
    )
```

time: 263 us -> 133 us (0.51)
  local copies, waits for them, and re-layouts: 82.8 us -> 16.5 us
  Pallas kernels: 0 us -> 50.2 us
  starting transfers between devices: 71.1 us -> 27.7 us
  waiting for transfers between devices: 70.3 us -> 35.3 us
  other arithmetic: 35.6 us -> 0.66 us
    scatter x3 -> x0, local copies, waits for them, and re-layouts: 66.2 us -> none  [the longest x1 58 us: body(): jnp.zeros((total_slots, 3, PARCEL_SITES), jnp.float32).at[flat_slot]]
    pallas_call x0 -> x7, Pallas kernels: none -> 50.2 us  [the longest x1 15.4 us: creep_of(): pl.pallas_call(creep_kernel, grid=(LANES // GROUP,), out_shape=jax.ShapeD...]
    all_to_all x4 -> x2, waiting for transfers between devices: 64.4 us -> 32.4 us  [exchange(): lax.all_to_all(x, ('gz', 'gy'), split_axis=0, concat_axis=0, tiled=True)]
    all_to_all x4 -> x2, starting transfers between devices: 39.9 us -> 15.4 us  [exchange(): lax.all_to_all(x, ('gz', 'gy'), split_axis=0, concat_axis=0, tiled=True)]
    select_n x8 -> x0, other arithmetic: 23.2 us -> none  [the longest x1 19.4 us: viscous_strain_advance(): series_result = jnp.where(placed[..., None, :], chain_new, series_prior)]
    ppermute x12 -> x4, starting transfers between devices: 31.2 us -> 12.3 us  [the longest x2 9.12 us: both_ways(): lax.ppermute(to_higher, axis, [(i, i + 1) for i in range(ends)])]
    unnamed x15 -> x26, local copies, waits for them, and re-layouts: 0.82 us -> 12 us
    slice x1 -> x0, local copies, waits for them, and re-layouts: 7.18 us -> none  [body(): got_fields[:, 1]]
  transfers between devices with their start and end apart: 16 -> 6, of which waited for: 4 -> 4; matrix products, arithmetic and copies ran while one was open for 32% -> 6% of each run, Pallas kernels for 0% -> 12%
where the time goes in v1:
time: 133 us; the launch traced here: 131 us
  Pallas kernels  50.2 us (38%)
  waiting for transfers between devices  35.3 us (27%)
  starting transfers between devices  27.7 us (21%)
  local copies, waits for them, and re-layouts  16.5 us (12%)
    all_to_all x2, waiting for transfers between devices, exchange(): lax.all_to_all(x, ('gz', 'gy'), split_axis=0, concat_axis=0, tiled=True)  32.4 us
    pallas_call x1, Pallas kernels, creep_of(): pl.pallas_call(creep_kernel, grid=(LANES // GROUP,), out_shape=jax.ShapeD...  15.4 us
    all_to_all x2, starting transfers between devices, exchange(): lax.all_to_all(x, ('gz', 'gy'), split_axis=0, concat_axis=0, tiled=True)  15.4 us
    pallas_call x1, Pallas kernels, states_of(): pl.pallas_call(state_kernel, grid=(LANES // GROUP,), out_shape=(jax.Shape...  13.2 us
    pallas_call x1, Pallas kernels, sweeps(): pl.pallas_call(sweep_kernel, out_shape=(grid_shape, grid_shape, grid_shap...  12.6 us
    unnamed x26, local copies, waits for them, and re-layouts  12 us
    ppermute x2, starting transfers between devices, both_ways(): lax.ppermute(to_higher, axis, [(i, i + 1) for i in range(ends)])  9.12 us
    pallas_call x1, Pallas kernels, collect(): pl.pallas_call(collect_kernel, out_shape=jax.ShapeDtypeStruct((ROWS, COLS...  3.58 us
  transfers between devices with their start and end apart: 6, of which 4 were waited for; matrix products, arithmetic and copies ran while one was open for 6% of the time, Pallas kernels for 12%

profile of v1, /device:TPU:1, one launch (start us, length us, event | category | flops | bytes accessed | tf_op | source)
XLA Modules:
  0.0 131.2 jit_solution(4935359978166213154)
XLA Ops:
  0.6 1.7 %shard_map.127 = (f32[144,128]{1,0:T(8,128)}, f32[144,128]{1,0:T(8,128)}) custom-call(f32[48,1536]{1,0:T(8,128)} %u_in.1, f32[48,1536]{1,0:T(8,128)} %u_in.1, f32[48,1536]{1,0:T(8,128)} %h_in.1, f32[48,1536]{1,0:T(8,128)} %h_in.1, f32[48,1536]{1,0:T(8,128)} %a_in.1, f32[48,1536]{1,0:T(8,128)} %a_in.1), custom_call_target="tpu_custom_call" | custom-call | tf_op jit(solution)/shard_map/pallas_call | solution.py:80
  2.3 4.0 %collective-permute-start = (f32[144,128]{1,0:T(8,128)}, f32[144,128]{1,0:T(8,128)S(1)}, u32[]{:S(2)}, u32[]{:S(2)}) collective-permute-start(f32[144,128]{1,0:T(8,128)} %get-tuple-element.16), channel_id=1, source_target_pairs={{0,1},{1,2},{2,3},{4,5},{5,6},{6,7},{8,9},{9,10},{10,11},{12,13},{... | collective-permute-start | bytes 221192 | tf_op jit(solution)/shard_map/ppermute | solution.py:479
  6.3 1.3 collective-permute-start.1
  7.6 1.4 %copy.19.keeper = s32[48,12]{1,0:T(8,128)} copy(s32[48,12]{0,1:T(8,128)} %param.12) | data formatting | bytes 4608 | tf_op args[4]
  9.0 0.8 copy.20.tally
  9.8 1.8 %collective-permute-done.1.from_right = f32[144,128]{1,0:T(8,128)S(1)} collective-permute-done((f32[144,128]{1,0:T(8,128)}, f32[144,128]{1,0:T(8,128)S(1)}, u32[]{:S(2)}, u32[]{:S(2)}) %collective-permute-start.1) | collective-permute-done | bytes 73760 | tf_op jit(solution)/shard_map/ppermute | solution.py:480
  12.3 1.8 %shard_map.128 = (f32[8,1920]{1,0:T(8,128)}, f32[8,1920]{1,0:T(8,128)}) custom-call(f32[48,1536]{1,0:T(8,128)} %u_in.1, f32[48,1536]{1,0:T(8,128)} %u_in.1, f32[48,1536]{1,0:T(8,128)} %h_in.1, f32[48,1536]{1,0:T(8,128)} %h_in.1, f32[48,1536]{1,0:T(8,128)} %a_in.1, f32[48,1536]{1,0:T(8,128)} %a_in.1, f32[144,128]{1,0:T(8,128)} %copy-done.4, f32[144,128]{1,0:T(8,128)} %copy-done.6), custom_call_target="tpu_custom_call" | custom-call | tf_op jit(solution)/shard_map/pallas_call | solution.py:129
  14.1 5.1 %collective-permute-start.2 = (f32[8,1920]{1,0:T(8,128)}, f32[8,1920]{1,0:T(8,128)S(1)}, u32[]{:S(2)}, u32[]{:S(2)}) collective-permute-start(f32[8,1920]{1,0:T(8,128)} %get-tuple-element.18), channel_id=1, source_target_pairs={{0,4},{4,8},{8,12},{12,16},{16,20},{20,24},{24,28},{28,32},{32,36}... | collective-permute-start | bytes 184328 | tf_op jit(solution)/shard_map/ppermute | solution.py:479
  19.2 1.9 %collective-permute-start.3 = (f32[8,1920]{1,0:T(8,128)}, f32[8,1920]{1,0:T(8,128)S(1)}, u32[]{:S(2)}, u32[]{:S(2)}) collective-permute-start(f32[8,1920]{1,0:T(8,128)} %get-tuple-element.19), channel_id=1, source_target_pairs={{4,0},{8,4},{12,8},{16,12},{20,16},{24,20},{28,24},{32,28},{36,32}... | collective-permute-start | bytes 184328 | tf_op jit(solution)/shard_map/ppermute | solution.py:480
  21.8 2.0 %shard_map.129.table = f32[128,128]{1,0:T(8,128)} custom-call(s32[4]{0:T(128)} %pad_add_fusion.place, s32[192]{0:T(256)} %times.1, s32[48,12]{1,0:T(8,128)} %copy.19.keeper), custom_call_target="tpu_custom_call" | custom-call | tf_op jit(solution)/shard_map/pallas_call | solution.py:160
  23.8 1.2 collective-permute-done.3.below
  24.9 1.0 copy-done
  25.9 1.0 copy-done.1
  26.9 1.0 copy-done.2
  27.8 0.7 copy-done.3
  28.6 0.9 copy-done.5
  29.4 0.9 copy-done.7
  30.3 0.8 copy-done.8
  31.2 0.7 copy-done.9
  31.8 12.6 %shard_map.130 = (f32[48,1536]{1,0:T(8,128)}, f32[48,1536]{1,0:T(8,128)}, f32[48,1536]{1,0:T(8,128)}, f32[4096,128]{1,0:T(8,128)}) custom-call(s32[4]{0:T(128)S(1)} %copy-done.9, s32[48,12]{1,0:T(8,128)S(1)} %copy-done.3, s32[48,12]{1,0:T(8,128)S(1)} %copy.20.tally, f32[48,1536]{1,0:T(8,128)S(1)} %copy-done, f32[48,1536]{1,0:T(8,128)S(1)} %copy-done.1, ...), custom_call_target="tpu_custom_call" | custom-call | tf_op jit(solution)/shard_map/pallas_call | solution.py:325
  44.4 11.5 %all-to-all-start = ((f32[128,32,128]{2,1,0:T(8,128)}), f32[128,32,128]{2,1,0:T(8,128)S(1)}, u32[]{:S(2)}, u32[]{:S(2)}) async-start(f32[128,32,128]{2,1,0:T(8,128)} %bitcast.2), calls=%async_computation | async-start | bytes 4194304 | tf_op jit(solution)/shard_map/all_to_all | solution.py:485
  56.0 1.3 reshape.28
  57.2 1.0 pad.4
  58.3 28.3 %all-to-all-done = f32[128,32,128]{2,1,0:T(8,128)S(1)} async-done(((f32[128,32,128]{2,1,0:T(8,128)}), f32[128,32,128]{2,1,0:T(8,128)S(1)}, u32[]{:S(2)}, u32[]{:S(2)}) %all-to-all-start) | async-done | bytes 2097184 | tf_op jit(solution)/shard_map/all_to_all | solution.py:485
  86.5 1.3 %copy-done.10 = f32[128,32,128]{2,1,0:T(8,128)} copy-done((f32[128,32,128]{2,1,0:T(8,128)}, f32[128,32,128]{2,1,0:T(8,128)S(1)}, u32[]{:S(2)}) %copy-start.10) | copy-done | bytes 2097176
  87.8 15.4 %shard_map.131 = f32[2048,128]{1,0:T(8,128)} custom-call(f32[4096,128]{1,0:T(8,128)} %bitcast.9, f32[1792,8,128]{2,1,0:T(8,128)} %chain.3, f32[2048,128]{1,0:T(8,128)} %bitcast.11), custom_call_target="tpu_custom_call" | custom-call | flops 36700160 | bytes 7340032 | tf_op jit(solution)/shard_map/pallas_call | solution.py:430
  103.3 3.8 %all-to-all-start.1 = ((f32[128,16,128]{2,1,0:T(8,128)}), f32[128,16,128]{2,1,0:T(8,128)S(1)}, u32[]{:S(2)}, u32[]{:S(2)}) async-start(f32[128,16,128]{2,1,0:T(8,128)} %bitcast.14), calls=%async_computation.1 | async-start | bytes 2097152 | tf_op jit(solution)/shard_map/all_to_all | solution.py:485
  107.1 13.2 %shard_map.133 = (f32[1792,8,128]{2,1,0:T(8,128)}, f32[2048,128]{1,0:T(8,128)}) custom-call(f32[4096,128]{1,0:T(8,128)} %bitcast.10, f32[1792,8,128]{2,1,0:T(8,128)} %chain.3, f32[2048,128]{1,0:T(8,128)} %bitcast.12), custom_call_target="tpu_custom_call" | custom-call | flops 36700160 | bytes 14680064 | tf_op jit(solution)/shard_map/pallas_call | solution.py:442
  120.3 2.2 %reshape.31 = f32[1792,128]{1,0:T(8,128)} reshape(f32[128,14,128]{2,1,0:T(8,128)} %bitcast.15) | data formatting | bytes 1835008 | tf_op jit(solution)/shard_map/reshape | solution.py:502
  122.5 4.1 %all-to-all-done.1 = f32[128,16,128]{2,1,0:T(8,128)S(1)} async-done(((f32[128,16,128]{2,1,0:T(8,128)}), f32[128,16,128]{2,1,0:T(8,128)S(1)}, u32[]{:S(2)}, u32[]{:S(2)}) %all-to-all-start.1) | async-done | bytes 1048608 | tf_op jit(solution)/shard_map/all_to_all | solution.py:485
  126.6 1.0 copy-done.11
  127.6 3.6 %shard_map.132 = f32[48,1536]{1,0:T(8,128)} custom-call(s32[48,12]{1,0:T(8,128)} %copy.19.keeper, f32[2048,128]{1,0:T(8,128)} %bitcast.13), custom_call_target="tpu_custom_call" | custom-call | tf_op jit(solution)/shard_map/pallas_call | solution.py:468
  (17 shorter events, 1.3 us)
Async XLA Ops:
  2.3 7.5 %collective-permute-start = (f32[144,128]{1,0:T(8,128)}, f32[144,128]{1,0:T(8,128)S(1)}, u32[]{:S(2)}, u32[]{:S(2)}) collective-permute-start(f32[144,128]{1,0:T(8,128)} %get-tuple-element.16), channel_id=1, source_target_pairs={{0,1},{1,2},{2,3},{4,5},{5,6},{6,7},{8,9},{9,10},{10,11},{12,13},{... | collective-permute-start | bytes 221192 | tf_op jit(solution)/shard_map/ppermute | solution.py:479
  6.3 5.3 %collective-permute-start.1 = (f32[144,128]{1,0:T(8,128)}, f32[144,128]{1,0:T(8,128)S(1)}, u32[]{:S(2)}, u32[]{:S(2)}) collective-permute-start(f32[144,128]{1,0:T(8,128)} %get-tuple-element.17), channel_id=1, source_target_pairs={{1,0},{2,1},{3,2},{5,4},{6,5},{7,6},{9,8},{10,9},{11,10},{13,12},{... | collective-permute-start | bytes 221192 | tf_op jit(solution)/shard_map/ppermute | solution.py:480
  9.8 1.8 %copy-start.4 = (f32[144,128]{1,0:T(8,128)}, f32[144,128]{1,0:T(8,128)S(1)}, u32[]{:S(2)}) copy-start(f32[144,128]{1,0:T(8,128)S(1)} %collective-permute-done.from_left) | copy-start | bytes 221188
  11.6 0.6 copy-start.6
  14.1 9.7 %collective-permute-start.2 = (f32[8,1920]{1,0:T(8,128)}, f32[8,1920]{1,0:T(8,128)S(1)}, u32[]{:S(2)}, u32[]{:S(2)}) collective-permute-start(f32[8,1920]{1,0:T(8,128)} %get-tuple-element.18), channel_id=1, source_target_pairs={{0,4},{4,8},{8,12},{12,16},{16,20},{20,24},{24,28},{28,32},{32,36}... | collective-permute-start | bytes 184328 | tf_op jit(solution)/shard_map/ppermute | solution.py:479
  19.2 5.8 %collective-permute-start.3 = (f32[8,1920]{1,0:T(8,128)}, f32[8,1920]{1,0:T(8,128)S(1)}, u32[]{:S(2)}, u32[]{:S(2)}) collective-permute-start(f32[8,1920]{1,0:T(8,128)} %get-tuple-element.19), channel_id=1, source_target_pairs={{4,0},{8,4},{12,8},{16,12},{20,16},{24,20},{28,24},{32,28},{36,32}... | collective-permute-start | bytes 184328 | tf_op jit(solution)/shard_map/ppermute | solution.py:480
  24.9 1.0 copy-start
  25.9 1.0 copy-start.1
  26.9 1.0 copy-start.2
  27.8 0.7 copy-start.3
  28.6 0.9 copy-start.5
  29.4 0.9 copy-start.7
  30.3 0.8 copy-start.8
  31.2 0.7 copy-start.9
  44.4 42.1 %all-to-all-start = ((f32[128,32,128]{2,1,0:T(8,128)}), f32[128,32,128]{2,1,0:T(8,128)S(1)}, u32[]{:S(2)}, u32[]{:S(2)}) async-start(f32[128,32,128]{2,1,0:T(8,128)} %bitcast.2), calls=%async_computation | async-start | bytes 4194304 | tf_op jit(solution)/shard_map/all_to_all | solution.py:485
  86.5 1.3 %copy-start.10 = (f32[128,32,128]{2,1,0:T(8,128)}, f32[128,32,128]{2,1,0:T(8,128)S(1)}, u32[]{:S(2)}) copy-start(f32[128,32,128]{2,1,0:T(8,128)S(1)} %all-to-all-done) | copy-start | bytes 6291460
  103.3 23.3 %all-to-all-start.1 = ((f32[128,16,128]{2,1,0:T(8,128)}), f32[128,16,128]{2,1,0:T(8,128)S(1)}, u32[]{:S(2)}, u32[]{:S(2)}) async-start(f32[128,16,128]{2,1,0:T(8,128)} %bitcast.14), calls=%async_computation.1 | async-start | bytes 2097152 | tf_op jit(solution)/shard_map/all_to_all | solution.py:485
  126.6 1.0 copy-start.11

commit v2 on v1

v2 whole, which is shorter than its diff:
```python
import functools
import math

import jax
import jax.numpy as jnp
from jax import lax
from jax.experimental import pallas as pl
from jax.experimental.pallas import tpu as pltpu
from jax.sharding import PartitionSpec as P

NX = 48
LANES = 128
LIFT = 8
CAP = 14
UNITS = 8
ROWS = 48
TILES = 12
COLS = TILES * LANES
WIDE = (TILES + 3) * LANES
OWN = 2 * LANES
SEND = 32
BACK = 16
AGE_ROW = 14

D0 = 0.05 + 0.95 / (1.0 + 5.0**16)

F32 = jnp.float32


def grant(mib):
    return pltpu.CompilerParams(vmem_limit_bytes=mib * 2**20)


def whole_grant(room):
    return pltpu.CompilerParams(vmem_limit_bytes=64 * 2**20 - room)


HBM = pl.BlockSpec(memory_space=pltpu.HBM)
VMEM = pl.BlockSpec(memory_space=pltpu.VMEM)
SMEM = pl.BlockSpec(memory_space=pltpu.SMEM)


def rate_of(u, h, a):
    q = 7.5 - 7.5 * h
    q = q * q
    return 0.05 * (1.0 - a) * jnp.exp(0.5 * u) / (1.0 + q * q)


def excess_diffusivity(h):
    p = 5.0 * (1.0 - h)
    p = p * p
    p = p * p
    p = p * p
    p = p * p
    return (0.05 - D0) + 0.95 / (1.0 + p)


def lanes_of(shape):
    return lax.broadcasted_iota(jnp.int32, shape, len(shape) - 1)


def split_position(p):
    owner = lax.shift_right_logical(p * 37450, 19)
    return owner, p - CAP * owner


def place_of(p, stride):
    return p + (stride - CAP) * lax.shift_right_logical(p * 37450, 19)


def start_all(pairs, sems):
    copies = [pltpu.make_async_copy(src, dst, sems.at[i]) for i, (src, dst) in enumerate(pairs)]
    for copy in copies:
        copy.start()
    return copies


def pack_y_kernel(u, h, a, to_left, to_right, left, right, sems):
    wide = 2 * LANES
    pairs = []
    for f, field in enumerate((u, h, a)):
        pairs.append((field.at[:, 0:wide], left.at[f]))
        pairs.append((field.at[:, COLS - wide : COLS], right.at[f]))
    for copy in start_all(pairs, sems):
        copy.wait()
    lane = lanes_of((ROWS, LANES))
    first, second = slice(0, LANES), slice(LANES, wide)
    to_left[0:ROWS, :] = left[0, :, first]
    to_left[ROWS : 2 * ROWS, :] = left[1, :, first]
    far_u = pltpu.roll(left[0, :, second], 96, 1)
    far_h = pltpu.roll(left[1, :, second], 112, 1)
    to_left[2 * ROWS : 3 * ROWS, :] = jnp.where(
        lane < 96, left[2, :, first], jnp.where(lane < 112, far_u, far_h)
    )
    to_right[0:ROWS, :] = right[0, :, second]
    to_right[ROWS : 2 * ROWS, :] = right[1, :, second]
    far_u = pltpu.roll(right[0, :, first], 16, 1)
    far_h = pltpu.roll(right[1, :, first], 32, 1)
    to_right[2 * ROWS : 3 * ROWS, :] = jnp.where(
        lane >= 32, right[2, :, second], jnp.where(lane < 16, far_u, far_h)
    )


def pack_y(u, h, a):
    shape = jax.ShapeDtypeStruct((3 * ROWS, LANES), F32)
    return pl.pallas_call(
        pack_y_kernel,
        out_shape=(shape, shape),
        in_specs=[HBM] * 3,
        out_specs=(VMEM, VMEM),
        scratch_shapes=[
            pltpu.VMEM((3, ROWS, 2 * LANES), F32),
            pltpu.VMEM((3, ROWS, 2 * LANES), F32),
            pltpu.SemaphoreType.DMA((6,)),
        ],
        compiler_params=whole_grant(288 * 2**10),
    )(u, h, a)


def side_tiles(from_left, from_right, lo, n):
    lane = lanes_of((n, LANES))
    rows = [slice(f * ROWS + lo, f * ROWS + lo + n) for f in range(3)]
    lx, rx = from_left[rows[2], :], from_right[rows[2], :]
    zero = jnp.zeros((n, LANES), F32)

    def far(left_shift, right_shift):
        return jnp.where(
            lane < 16,
            pltpu.roll(rx, right_shift, 1),
            jnp.where(lane >= 112, pltpu.roll(lx, left_shift, 1), zero),
        )

    return (
        (far(112, 32), from_left[rows[0], :], from_right[rows[0], :]),
        (far(96, 16), from_left[rows[1], :], from_right[rows[1], :]),
        (zero, jnp.where(lane >= 32, lx, zero), jnp.where(lane < 96, rx, zero)),
    )


Z_SHIFTS = (("up", 0, (0, 3, 6)), ("down", ROWS - 8, (3, 6, 0)))


def three_fields(fields, shifts):
    u, h, a = [pltpu.roll(v, s, 0) if s else v for v, s in zip(fields, shifts)]
    row = lax.broadcasted_iota(jnp.int32, u.shape, 0)
    return jnp.where(row < 3, u, jnp.where(row < 6, h, a))


def pack_z_kernel(up_own, down_own, from_left, from_right, up, down):
    for out, own, (_, lo, shifts) in zip((up, down), (up_own, down_own), Z_SHIFTS):
        sides = side_tiles(from_left, from_right, lo, 8)
        out[:, OWN : OWN + COLS] = own[...]
        for t, at in enumerate((0, LANES, OWN + COLS)):
            out[:, at : at + LANES] = three_fields([side[t] for side in sides], shifts)


def pack_z(up_own, down_own, from_left, from_right):
    shape = jax.ShapeDtypeStruct((8, WIDE), F32)
    return pl.pallas_call(
        pack_z_kernel,
        out_shape=(shape, shape),
        in_specs=[VMEM] * 4,
        out_specs=(VMEM, VMEM),
        compiler_params=grant(4),
    )(up_own, down_own, from_left, from_right)


def prepare_kernel(place, times, keeper, u, h, a, table, up, down, ends, sems):
    pairs = []
    for f, field in enumerate((u, h, a)):
        pairs.append((field.at[0:8, :], ends.at[0, f]))
        pairs.append((field.at[ROWS - 8 : ROWS, :], ends.at[1, f]))
    copies = start_all(pairs, sems)
    lane = lanes_of((ROWS, LANES))
    solid = []
    for r in range(ROWS // LIFT):
        age = 2400.0 - jnp.full((LIFT, LANES), times[place[0] * (ROWS // LIFT) + r], jnp.int32).astype(F32)
        solid.append(jnp.sqrt(600.0 / age) + 0.2)
    solid = jnp.concatenate(solid, axis=0)
    owners, slots = [], []
    positions = jnp.transpose(keeper[...])
    for j in range(TILES):
        owner, slot = split_position(jnp.broadcast_to(positions[:, j : j + 1], (ROWS, LANES)))
        owners.append(jnp.where(owner == lane, 1.0, 0.0))
        slots.append(jnp.where(slot == lane, solid, 0.0))
    table[...] = lax.dot_general(
        jnp.concatenate(owners, axis=0),
        jnp.concatenate(slots, axis=0),
        (((0,), (0,)), ((), ())),
        precision=lax.Precision.HIGHEST,
        preferred_element_type=F32,
    )
    for copy in copies:
        copy.wait()
    for out, e, (_, _, shifts) in zip((up, down), (0, 1), Z_SHIFTS):
        out[...] = three_fields([ends[e, f] for f in range(3)], shifts)


def prepare(place, times, keeper, u, h, a):
    rows = jax.ShapeDtypeStruct((8, COLS), F32)
    return pl.pallas_call(
        prepare_kernel,
        out_shape=(jax.ShapeDtypeStruct((LANES, LANES), F32), rows, rows),
        in_specs=[SMEM, SMEM, VMEM] + [HBM] * 3,
        out_specs=[VMEM] * 3,
        scratch_shapes=[pltpu.VMEM((2, 3, 8, COLS), F32), pltpu.SemaphoreType.DMA((6,))],
        compiler_params=whole_grant(544 * 2**10),
    )(place, times, keeper, u, h, a)


def sweep_kernel(
    place,
    keeper,
    tally,
    u_in,
    h_in,
    a_in,
    from_left,
    from_right,
    above,
    below,
    table,
    t_hbm,
    h_hbm,
    m_hbm,
    send_hbm,
    u_first,
    h_first,
    a_wide,
    fields,
    phi_buf,
    load_buf,
    tally_buf,
    t_out,
    h_out,
    m_out,
    send,
    sems,
):
    gz, gy, last_z, last_y = place[0], place[1], place[2], place[3]
    tiles = ROWS // 8 + 1

    own_cells = (slice(0, ROWS), slice(OWN, OWN + COLS))
    loads = start_all(
        [(src, wide.at[own_cells]) for src, wide in ((u_in, u_first), (h_in, h_first), (a_in, a_wide))],
        sems,
    )

    send[...] = jnp.zeros_like(send)
    for o in range(LANES):
        send[o * SEND + AGE_ROW : o * SEND + AGE_ROW + 1, :] = table[o : o + 1, :]

    sides = side_tiles(from_left, from_right, 0, ROWS)
    for wide, side in zip((u_first, h_first, a_wide), sides):
        wide[0:ROWS, 0:LANES] = side[0]
        wide[0:ROWS, LANES:OWN] = side[1]
        wide[0:ROWS, OWN + COLS : WIDE] = side[2]
    row8 = lax.broadcasted_iota(jnp.int32, (8, WIDE), 0)
    zero = jnp.zeros((8, WIDE), F32)
    top, bottom = above[...], below[...]
    for wide, down_shift, up_shift in ((u_first, 0, 5), (h_first, 5, 2), (a_wide, 2, 0)):
        b = pltpu.roll(bottom, down_shift, 0) if down_shift else bottom
        t = pltpu.roll(top, up_shift, 0) if up_shift else top
        wide[ROWS : ROWS + 8, :] = jnp.where(row8 < 3, b, jnp.where(row8 >= 5, t, zero))

    column = lanes_of((8, WIDE))
    line = lax.rem(column + (16 * NX - OWN), NX)
    not_first, not_last = line != 0, line != NX - 1
    on_left = (column >= 64) & (column < OWN)
    on_own = (column >= OWN) & (column < OWN + COLS)
    left_is, right_is = (gy > 0).astype(jnp.int32), (gy < last_y).astype(jnp.int32)
    above_is, below_is = (gz > 0).astype(jnp.int32), (gz < last_z).astype(jnp.int32)
    inside_columns = jnp.where(on_own, 1, jnp.where(on_left, left_is, right_is))

    def derived(h):
        d = excess_diffusivity(h)
        return d, d * h

    for copy in loads:
        copy.wait()

    def fill(r, carry):
        rows = pl.ds(pl.multiple_of(r * 8, 8), 8)
        h = h_first[rows, :]
        d, dh = derived(h)
        fields[0, 0, rows, :] = u_first[rows, :]
        fields[0, 1, rows, :] = h
        fields[0, 2, rows, :] = d
        fields[0, 3, rows, :] = dh
        return carry

    lax.fori_loop(0, tiles, fill, 0)

    def step(src, r):
        here = pl.ds(pl.multiple_of(r * 8, 8), 8)
        before = pl.ds(pl.multiple_of(jnp.where(r == 0, tiles - 1, r - 1) * 8, 8), 8)
        after = pl.ds(pl.multiple_of(jnp.where(r == tiles - 1, 0, r + 1) * 8, 8), 8)

        def around(f):
            v = fields[src, f, here, :]
            lower, upper = fields[src, f, before, :], fields[src, f, after, :]
            total = pltpu.roll(jnp.where(row8 == 0, upper, v), 7, 0)
            total = total + pltpu.roll(jnp.where(row8 == 7, lower, v), 1, 0)
            total = total + pltpu.roll(v, WIDE - NX, 1)
            total = total + pltpu.roll(v, NX, 1)
            total = total + pltpu.roll(jnp.where(not_first, v, 0.0), WIDE - 1, 1)
            total = total + pltpu.roll(jnp.where(not_last, v, 0.0), 1, 1)
            return total

        u, h, d = fields[src, 0, here, :], fields[src, 1, here, :], fields[src, 2, here, :]
        r_now = rate_of(u, h, a_wide[here, :])
        u_next = (u_first[here, :] + 4.0 * r_now + around(0)) * (1.0 / 7.0)
        conduct = 3.0 * (d + 2.0 * D0) + 0.5 * around(2)
        inflow = 0.5 * ((d + 2.0 * D0) * around(1) + around(3))
        h_next = (h_first[here, :] - 0.5 * r_now + inflow) / (1.0 + conduct)
        return u_next, h_next

    def middle(src):
        def run(r, carry):
            rows = pl.ds(pl.multiple_of(r * 8, 8), 8)
            u, h = step(src, r)
            own_rows = (r < tiles - 1).astype(jnp.int32)
            below_in, above_in = jnp.maximum(own_rows, below_is), jnp.maximum(own_rows, above_is)
            keep = inside_columns * jnp.where(row8 < 4, below_in, above_in) > 0
            u, h = jnp.where(keep, u, 0.0), jnp.where(keep, h, 0.0)
            d, dh = derived(h)
            fields[1 - src, 0, rows, :] = u
            fields[1 - src, 1, rows, :] = h
            fields[1 - src, 2, rows, :] = d
            fields[1 - src, 3, rows, :] = dh
            return carry

        lax.fori_loop(0, tiles, run, 0)

    middle(0)
    middle(1)

    lane8 = lanes_of((8, LANES))

    counts_t = jnp.transpose(tally[...])
    for r in range(tiles - 1):
        tally_buf[r * 8 : (r + 1) * 8, 0:TILES] = counts_t[r * 8 : (r + 1) * 8, :]

    def last(r, carry):
        rows = pl.ds(pl.multiple_of(r * 8, 8), 8)
        u, h = step(0, r)
        u, h = u[:, OWN : OWN + COLS], h[:, OWN : OWN + COLS]
        a = a_wide[rows, OWN : OWN + COLS]
        m = a + rate_of(u, h, a)
        t_out[rows, :] = u
        h_out[rows, :] = h
        m_out[rows, :] = m
        load = -m * (0.075 * u + 0.3 * (1.0 - h))
        phi = jnp.exp(0.3 * u) * (0.1 + 0.9 * h * h)
        counts = tally_buf[rows, :]
        for j in range(TILES):
            part = slice(j * LANES, (j + 1) * LANES)
            placed = lane8 < jnp.broadcast_to(counts[:, j : j + 1], (8, LANES))
            block_rows = pl.ds(pl.multiple_of(j * ROWS + r * 8, 8), 8)
            phi_buf[block_rows, :] = jnp.where(placed, phi[:, part], 0.0)
            load_buf[block_rows, :] = load[:, part]
        return carry

    lax.fori_loop(0, tiles - 1, last, 0)

    results = start_all([(t_out, t_hbm), (h_out, h_hbm), (m_out, m_hbm)], sems)

    def scatter(z, carry):
        for j in range(TILES):
            at = place_of(keeper[j, z], SEND)
            block = pl.ds(j * ROWS + z, 1)
            send[pl.ds(at, 1), :] = phi_buf[block, :]
            send[pl.ds(at + 16, 1), :] = load_buf[block, :]
        return carry

    lax.fori_loop(0, ROWS, scatter, 0)
    message = pltpu.make_async_copy(send, send_hbm, sems.at[3])
    message.start()
    for copy in results:
        copy.wait()
    message.wait()


def sweeps(place, keeper, tally, u, h, a, from_left, from_right, above, below, table):
    grid_shape = jax.ShapeDtypeStruct((ROWS, COLS), F32)
    wide = pltpu.VMEM((ROWS + 8, WIDE), F32)
    return pl.pallas_call(
        sweep_kernel,
        out_shape=(grid_shape, grid_shape, grid_shape, jax.ShapeDtypeStruct((LANES * SEND, LANES), F32)),
        in_specs=[SMEM, SMEM, VMEM] + [HBM] * 3 + [VMEM] * 5,
        out_specs=[HBM] * 4,
        scratch_shapes=[
            wide,
            wide,
            wide,
            pltpu.VMEM((2, 4, ROWS + 8, WIDE), F32),
            pltpu.VMEM((TILES * ROWS, LANES), F32),
            pltpu.VMEM((TILES * ROWS, LANES), F32),
            pltpu.VMEM((ROWS, LANES), jnp.int32),
            pltpu.VMEM((ROWS, COLS), F32),
            pltpu.VMEM((ROWS, COLS), F32),
            pltpu.VMEM((ROWS, COLS), F32),
            pltpu.VMEM((LANES * SEND, LANES), F32),
            pltpu.SemaphoreType.DMA((4,)),
        ],
        compiler_params=whole_grant(544 * 2**10),
    )(place, keeper, tally, u, h, a, from_left, from_right, above, below, table)


GROUP = 16
PARTS = LANES // GROUP


def decay_rates():
    unit = lax.broadcasted_iota(jnp.int32, (UNITS, LANES), 0)
    scale = jnp.zeros((UNITS, LANES), F32)
    for m in range(UNITS):
        scale = jnp.where(unit == m, -math.log2(math.e) / (0.1 * 3.0**m), scale)
    return scale


def unit_change(prior, got, at, scale):
    phi = jnp.broadcast_to(got[pl.ds(at, 1), :], (UNITS, LANES))
    load = jnp.broadcast_to(got[pl.ds(at + 16, 1), :], (UNITS, LANES))
    return (1.0 - jnp.exp2(phi * scale)) * (load - prior)


def sum_units(parts):
    row = lax.broadcasted_iota(jnp.int32, (8, LANES), 0)
    low = row < 4
    pairs = []
    for k in range(4):
        x, y = parts[k], parts[k + 4]
        pairs.append(jnp.where(low, x, y) + pltpu.roll(jnp.where(low, y, x), 4, 0))
    for step in (2, 1):
        first = (row & step) == 0
        pairs = [
            jnp.where(
                first,
                pairs[k] + pltpu.roll(pairs[k], 8 - step, 0),
                pairs[k + step] + pltpu.roll(pairs[k + step], step, 0),
            )
            for k in range(step)
        ]
    return pairs[0]


def load_states(chain_hbm, tension_hbm, chain, tension, sems):
    n = GROUP * CAP
    pairs = [(tension_hbm, tension.at[0 : LANES * CAP])]
    pairs += [(chain_hbm.at[i * n : (i + 1) * n], chain.at[i * n : (i + 1) * n]) for i in range(PARTS)]
    return start_all(pairs, sems)


def creep_kernel(got, chain_hbm, tension_hbm, creep_hbm, chain, tension, creep, in_sems, out_sems):
    loads = load_states(chain_hbm, tension_hbm, chain, tension, in_sems)
    scale = decay_rates()
    diagonal = lanes_of((BACK, LANES)) == lax.broadcasted_iota(jnp.int32, (BACK, LANES), 0)

    def one(s, carry):
        base = pl.multiple_of(s * SEND, SEND)
        ages = jnp.broadcast_to(got[pl.ds(base + AGE_ROW, 1), :], (BACK, LANES))
        solid = jnp.sum(jnp.where(diagonal, ages, 0.0), axis=1, keepdims=True)
        zero = jnp.zeros((UNITS, LANES), F32)
        changes = [unit_change(chain[s * CAP + k], got, base + k, scale) for k in range(CAP)]
        changes += [zero] * (BACK - CAP)
        total = jnp.concatenate([sum_units(changes[:8]), sum_units(changes[8:])], axis=0)
        rows = pl.ds(pl.multiple_of(s * BACK, BACK), BACK)
        phi, load = got[pl.ds(base, 16), :], got[pl.ds(base + 16, 16), :]
        before = tension[pl.ds(s * CAP, BACK), :]
        after = before / (1.0 + 0.2 * phi * before)
        creep[rows, :] = solid * total + (0.1 / 0.15) * phi * after * load
        return carry

    tension[LANES * CAP :, :] = jnp.ones((BACK, LANES), F32)
    loads[0].wait()
    stores = []
    for i in range(PARTS):
        loads[1 + i].wait()
        lax.fori_loop(i * GROUP, (i + 1) * GROUP, one, 0, unroll=2)
        part = slice(i * GROUP * BACK, (i + 1) * GROUP * BACK)
        stores.append(pltpu.make_async_copy(creep.at[part], creep_hbm.at[part], out_sems.at[i]))
        stores[-1].start()
    for copy in stores:
        copy.wait()


def state_kernel(got, chain_hbm, tension_hbm, chain_new, tension_new, chain, tension, in_sems, out_sems):
    loads = load_states(chain_hbm, tension_hbm, chain, tension, in_sems)
    scale = decay_rates()
    used = lax.broadcasted_iota(jnp.int32, (BACK, LANES), 0) < CAP

    def one(s, carry):
        base = pl.multiple_of(s * SEND, SEND)
        for k in range(CAP):
            prior = chain[s * CAP + k]
            chain[s * CAP + k] = prior + unit_change(prior, got, base + k, scale)
        phi = got[pl.ds(base, 16), :]
        rows = pl.ds(s * CAP, BACK)
        before = tension[rows, :]
        tension[rows, :] = jnp.where(used, before / (1.0 + 0.2 * phi * before), before)
        return carry

    tension[LANES * CAP :, :] = jnp.ones((BACK, LANES), F32)
    loads[0].wait()
    stores = []
    n = GROUP * CAP
    for i in range(PARTS):
        loads[1 + i].wait()
        lax.fori_loop(i * GROUP, (i + 1) * GROUP, one, 0)
        part = slice(i * n, (i + 1) * n)
        stores.append(pltpu.make_async_copy(chain.at[part], chain_new.at[part], out_sems.at[i]))
        stores[-1].start()
    stores.append(pltpu.make_async_copy(tension.at[0 : LANES * CAP], tension_new, out_sems.at[PARTS]))
    stores[-1].start()
    for copy in stores:
        copy.wait()


def owner_scratch(creep):
    return [
        pltpu.VMEM((LANES * CAP, UNITS, LANES), F32),
        pltpu.VMEM((LANES * CAP + BACK, LANES), F32),
        *creep,
        pltpu.SemaphoreType.DMA((PARTS + 1,)),
        pltpu.SemaphoreType.DMA((PARTS + 1,)),
    ]


def creep_of(got, chain, tension):
    shape = (LANES * BACK, LANES)
    return pl.pallas_call(
        creep_kernel,
        out_shape=jax.ShapeDtypeStruct(shape, F32),
        in_specs=[VMEM, HBM, HBM],
        out_specs=HBM,
        scratch_shapes=owner_scratch([pltpu.VMEM(shape, F32)]),
        compiler_params=whole_grant(2560 * 2**10),
        cost_estimate=pl.CostEstimate(flops=20 * chain.size, bytes_accessed=4 * chain.size, transcendentals=chain.size),
    )(got, chain, tension)


def states_of(got, chain, tension):
    return pl.pallas_call(
        state_kernel,
        out_shape=(jax.ShapeDtypeStruct(chain.shape, F32), jax.ShapeDtypeStruct(tension.shape, F32)),
        in_specs=[VMEM, HBM, HBM],
        out_specs=(HBM, HBM),
        scratch_shapes=owner_scratch([]),
        compiler_params=whole_grant(2560 * 2**10),
        cost_estimate=pl.CostEstimate(flops=20 * chain.size, bytes_accessed=8 * chain.size, transcendentals=chain.size),
    )(got, chain, tension)


def collect_kernel(keeper, back, out, blocks):
    def line(z, carry):
        for j in range(TILES):
            at = place_of(keeper[j, z], BACK)
            blocks[pl.ds(j * ROWS + z, 1), :] = back[pl.ds(at, 1), :]
        return carry

    lax.fori_loop(0, ROWS, line, 0)
    for j in range(TILES):
        out[:, j * LANES : (j + 1) * LANES] = blocks[j * ROWS : (j + 1) * ROWS, :]


def collect(keeper, back):
    return pl.pallas_call(
        collect_kernel,
        out_shape=jax.ShapeDtypeStruct((ROWS, COLS), F32),
        in_specs=[SMEM, VMEM],
        out_specs=VMEM,
        scratch_shapes=[pltpu.VMEM((TILES * ROWS, LANES), F32)],
        compiler_params=grant(4),
    )(keeper, back)


def both_ways(axis, to_lower, to_higher):
    ends = lax.axis_size(axis) - 1
    from_lower = lax.ppermute(to_higher, axis, [(i, i + 1) for i in range(ends)])
    from_higher = lax.ppermute(to_lower, axis, [(i + 1, i) for i in range(ends)])
    return from_lower, from_higher


def exchange(x):
    return lax.all_to_all(x, ("gz", "gy"), split_axis=0, concat_axis=0, tiled=True)


def body(u, h, a, tally, keeper, times, chain, tension):
    ends = [jnp.int32(lax.axis_size(n) - 1) for n in ("gz", "gy")]
    place = jnp.stack([lax.axis_index("gz"), lax.axis_index("gy"), *ends]).astype(jnp.int32)
    tally, keeper = tally.T, keeper.T
    to_left, to_right = pack_y(u, h, a)
    from_left, from_right = both_ways("gy", to_left, to_right)
    table, up_own, down_own = prepare(place, times, keeper, u, h, a)
    up, down = pack_z(up_own, down_own, from_left, from_right)
    above, below = both_ways("gz", up, down)
    t_new, h_new, m_new, send = sweeps(place, keeper, tally, u, h, a, from_left, from_right, above, below, table)
    got = exchange(send)
    creep = creep_of(got, chain, tension)
    back = exchange(creep)
    chain_new, tension_new = states_of(got, chain, tension)
    return t_new, h_new, m_new, collect(keeper, back), chain_new, tension_new


def solution(mesh):
    grid = P("gz", "gy")
    owners = ("gz", "gy")
    return jax.shard_map(
        body,
        mesh=mesh,
        in_specs=(grid, grid, grid, grid, grid, P(), P(owners, None, None), P(owners, None)),
        out_specs=(grid, grid, grid, grid, P(owners, None, None), P(owners, None)),
        check_vma=False,
    )
```

time: 133 us -> 116 us (0.87)
  blocking collectives: 0 us -> 42.2 us
  waiting for transfers between devices: 35.3 us -> 16 us
  local copies, waits for them, and re-layouts: 16.5 us -> 2.25 us
  Pallas kernels: 50.2 us -> 37.4 us
  starting transfers between devices: 27.7 us -> 16.2 us
    all_to_all x0 -> x1, blocking collectives: none -> 42.2 us  [exchange(): lax.all_to_all(x, ('gz', 'gy'), split_axis=0, concat_axis=0, tiled=True)]
    all_to_all x2 -> x1, waiting for transfers between devices: 32.4 us -> 11.3 us  [exchange(): lax.all_to_all(x, ('gz', 'gy'), split_axis=0, concat_axis=0, tiled=True)]
    pallas_call x5, Pallas kernels: 34.1 us -> 21.4 us  [the longest x1 9.17 us: creep_of(): pl.pallas_call(creep_kernel, out_shape=jax.ShapeDtypeStruct(shape, F32),...]
    all_to_all x2 -> x1, starting transfers between devices: 15.4 us -> 3.82 us  [exchange(): lax.all_to_all(x, ('gz', 'gy'), split_axis=0, concat_axis=0, tiled=True)]
    unnamed x26 -> x14, local copies, waits for them, and re-layouts: 12 us -> 2.25 us
    reshape x2 -> x0, local copies, waits for them, and re-layouts: 3.48 us -> none  [the longest x1 2.21 us: body(): tension_new.reshape(LANES, BACK, LANES)[:, :CAP].reshape(-1, LANES)]
    ppermute x2, waiting for transfers between devices: 2.98 us -> 4.62 us  [both_ways(): lax.ppermute(to_lower, axis, [(i + 1, i) for i in range(ends)])]
  transfers between devices with their start and end apart: 6 -> 5, of which waited for: 4 -> 3; matrix products, arithmetic and copies ran while one was open for 6% -> 1% of each run, Pallas kernels for 12% -> 9%
where the time goes in v2:
time: 116 us; the launch traced here: 115 us
  blocking collectives  42.2 us (36%)
  Pallas kernels  37.4 us (32%)
  starting transfers between devices  16.2 us (14%)
  waiting for transfers between devices  16 us (14%)
  local copies, waits for them, and re-layouts  2.25 us (2%)
    all_to_all x1, blocking collectives, exchange(): lax.all_to_all(x, ('gz', 'gy'), split_axis=0, concat_axis=0, tiled=True)  42.2 us
    pallas_call x1, Pallas kernels, sweeps(): pl.pallas_call(sweep_kernel, out_shape=(grid_shape, grid_shape, grid_shap...  13.1 us
    all_to_all x1, waiting for transfers between devices, exchange(): lax.all_to_all(x, ('gz', 'gy'), split_axis=0, concat_axis=0, tiled=True)  11.3 us
    pallas_call x1, Pallas kernels, creep_of(): pl.pallas_call(creep_kernel, out_shape=jax.ShapeDtypeStruct(shape, F32),...  9.17 us
    ppermute x2, starting transfers between devices, both_ways(): lax.ppermute(to_higher, axis, [(i, i + 1) for i in range(ends)])  9.14 us
    pallas_call x1, Pallas kernels, states_of(): pl.pallas_call(state_kernel, out_shape=(jax.ShapeDtypeStruct(chain.shape,...  8.14 us
    ppermute x2, waiting for transfers between devices, both_ways(): lax.ppermute(to_lower, axis, [(i + 1, i) for i in range(ends)])  4.62 us
    all_to_all x1, starting transfers between devices, exchange(): lax.all_to_all(x, ('gz', 'gy'), split_axis=0, concat_axis=0, tiled=True)  3.82 us
  transfers between devices with their start and end apart: 5, of which 3 were waited for; matrix products, arithmetic and copies ran while one was open for 1% of the time, Pallas kernels for 9%

profile of v2, /device:TPU:1, one launch (start us, length us, event | category | flops | bytes accessed | tf_op | source)
XLA Modules:
  0.0 115.4 jit_solution(17890144221660062429)
XLA Ops:
  0.6 1.7 %shard_map.127 = (f32[144,128]{1,0:T(8,128)}, f32[144,128]{1,0:T(8,128)}) custom-call(f32[48,1536]{1,0:T(8,128)} %u_in.1, f32[48,1536]{1,0:T(8,128)} %h_in.1, f32[48,1536]{1,0:T(8,128)} %a_in.1), custom_call_target="tpu_custom_call" | custom-call | tf_op jit(solution)/shard_map/pallas_call | solution.py:106
  2.3 4.0 %collective-permute-start = (f32[144,128]{1,0:T(8,128)}, f32[144,128]{1,0:T(8,128)S(1)}, u32[]{:S(2)}, u32[]{:S(2)}) collective-permute-start(f32[144,128]{1,0:T(8,128)} %get-tuple-element.19), channel_id=1, source_target_pairs={{0,1},{1,2},{2,3},{4,5},{5,6},{6,7},{8,9},{9,10},{10,11},{12,13},{... | collective-permute-start | bytes 221192 | tf_op jit(solution)/shard_map/ppermute | solution.py:580
  6.4 1.3 %collective-permute-start.1 = (f32[144,128]{1,0:T(8,128)}, f32[144,128]{1,0:T(8,128)S(1)}, u32[]{:S(2)}, u32[]{:S(2)}) collective-permute-start(f32[144,128]{1,0:T(8,128)} %get-tuple-element.20), channel_id=1, source_target_pairs={{1,0},{2,1},{3,2},{5,4},{6,5},{7,6},{9,8},{10,9},{11,10},{13,12},{... | collective-permute-start | bytes 221192 | tf_op jit(solution)/shard_map/ppermute | solution.py:581
  7.7 0.6 pad_add_fusion.place
  8.3 2.3 %shard_map.128 = (f32[128,128]{1,0:T(8,128)}, f32[8,1536]{1,0:T(8,128)}, f32[8,1536]{1,0:T(8,128)}) custom-call(s32[4]{0:T(128)} %pad_add_fusion.place, s32[192]{0:T(256)} %times.1, s32[12,48]{1,0:T(8,128)} %bitcast.9, f32[48,1536]{1,0:T(8,128)} %u_in.1, f32[48,1536]{1,0:T(8,128)} %h_in.1, f32[48,1536]{1,0:T(8,128)} %a_in.1), custom_call_target="tpu_custom_call" | custom-call | tf_op jit(solution)/shard_map/pallas_call | solution.py:201
  10.7 0.0 collective-permute-done.from_left
  10.7 0.0 copy-start
  10.7 1.0 collective-permute-done.1.from_right
  11.7 0.0 copy-start.1
  11.7 0.0 copy-start.3
  11.7 0.8 copy-done.3
  12.5 0.8 copy-done.4
  13.3 0.1 shard_map.129
  13.4 5.1 %collective-permute-start.2 = (f32[8,1920]{1,0:T(8,128)S(1)}, f32[8,1920]{1,0:T(8,128)S(1)}, u32[]{:S(2)}, u32[]{:S(2)}) collective-permute-start(f32[8,1920]{1,0:T(8,128)S(1)} %get-tuple-element.23), channel_id=1, source_target_pairs={{0,4},{4,8},{8,12},{12,16},{16,20},{20,24},{24,28},{28,32},{32,36}... | collective-permute-start | bytes 184328 | tf_op jit(solution)/shard_map/ppermute | solution.py:580
  18.5 1.9 %collective-permute-start.3 = (f32[8,1920]{1,0:T(8,128)S(1)}, f32[8,1920]{1,0:T(8,128)S(1)}, u32[]{:S(2)}, u32[]{:S(2)}) collective-permute-start(f32[8,1920]{1,0:T(8,128)S(1)} %get-tuple-element.24), channel_id=1, source_target_pairs={{4,0},{8,4},{12,8},{16,12},{20,16},{24,20},{28,24},{32,28},{36,32}... | collective-permute-start | bytes 184328 | tf_op jit(solution)/shard_map/ppermute | solution.py:581
  20.4 0.0 collective-permute-done.2.above
  20.5 0.0 copy-start.5
  20.5 3.6 %collective-permute-done.3.below = f32[8,1920]{1,0:T(8,128)S(1)} collective-permute-done((f32[8,1920]{1,0:T(8,128)S(1)}, f32[8,1920]{1,0:T(8,128)S(1)}, u32[]{:S(2)}, u32[]{:S(2)}) %collective-permute-start.3) | collective-permute-done | bytes 61472 | tf_op jit(solution)/shard_map/ppermute | solution.py:581
  24.1 0.0 copy-start.6
  24.1 0.0 copy-done
  24.1 0.0 copy-done.1
  24.1 0.0 copy-done.5
  24.1 0.6 copy-done.6
  24.7 13.1 %shard_map.130 = (f32[48,1536]{1,0:T(8,128)}, f32[48,1536]{1,0:T(8,128)}, f32[48,1536]{1,0:T(8,128)}, f32[4096,128]{1,0:T(8,128)}) custom-call(s32[4]{0:T(128)} %pad_add_fusion.place, s32[12,48]{1,0:T(8,128)} %bitcast.10, s32[12,48]{1,0:T(8,128)} %bitcast.16, f32[48,1536]{1,0:T(8,128)} %u_in.1, f32[48,1536]{1,0:T(8,128)} %h_in.1, f32[48,1536]{1,0:T(8,128)} %a_in.1, ...), custom_call_target="tpu_custom_call" | custom-call | tf_op jit(solution)/shard_map/pallas_call | solution.py:387
  37.8 42.2 %all_to_all.22 = f32[128,32,128]{2,1,0:T(8,128)} all-to-all(f32[128,32,128]{2,1,0:T(8,128)} %bitcast.15), channel_id=1, replica_groups=mesh['gz'=32,'gy'=4] {'gz','gy'}, dimensions={0} | all-to-all | bytes 4194304 | tf_op jit(solution)/shard_map/all_to_all | solution.py:586
  80.0 9.2 %shard_map.131 = f32[2048,128]{1,0:T(8,128)} custom-call(f32[4096,128]{1,0:T(8,128)} %bitcast.12, f32[1792,8,128]{2,1,0:T(8,128)} %chain_hbm.3, f32[1792,128]{1,0:T(8,128)} %tension_hbm.3), custom_call_target="tpu_custom_call" | custom-call | flops 36700160 | bytes 7340032 | tf_op jit(solution)/shard_map/pallas_call | solution.py:532
  89.2 0.0 copy-start.2
  89.2 3.8 %all-to-all-start.1 = ((f32[128,16,128]{2,1,0:T(8,128)}), f32[128,16,128]{2,1,0:T(8,128)S(1)}, u32[]{:S(2)}, u32[]{:S(2)}) async-start(f32[128,16,128]{2,1,0:T(8,128)} %bitcast.14), calls=%async_computation.1 | async-start | bytes 2097152 | tf_op jit(solution)/shard_map/all_to_all | solution.py:586
  93.0 8.1 %shard_map.133 = (f32[1792,8,128]{2,1,0:T(8,128)}, f32[1792,128]{1,0:T(8,128)}) custom-call(f32[4096,128]{1,0:T(8,128)} %bitcast.13, f32[1792,8,128]{2,1,0:T(8,128)} %chain_hbm.3, f32[1792,128]{1,0:T(8,128)} %tension_hbm.3), custom_call_target="tpu_custom_call" | custom-call | flops 36700160 | bytes 14680064 | tf_op jit(solution)/shard_map/pallas_call | solution.py:544
  101.2 11.3 %all-to-all-done.1 = f32[128,16,128]{2,1,0:T(8,128)S(1)} async-done(((f32[128,16,128]{2,1,0:T(8,128)}), f32[128,16,128]{2,1,0:T(8,128)S(1)}, u32[]{:S(2)}, u32[]{:S(2)}) %all-to-all-start.1) | async-done | bytes 1048608 | tf_op jit(solution)/shard_map/all_to_all | solution.py:586
  112.5 0.0 copy-done.2
  112.5 2.9 %shard_map.132 = f32[48,1536]{1,0:T(8,128)} custom-call(s32[12,48]{1,0:T(8,128)S(1)} %bitcast.11, f32[2048,128]{1,0:T(8,128)S(1)} %bitcast.8), custom_call_target="tpu_custom_call" | custom-call | tf_op jit(solution)/shard_map/pallas_call | solution.py:568
  (1 shorter events, 0.0 us)
Async XLA Ops:
  2.3 8.3 %collective-permute-start = (f32[144,128]{1,0:T(8,128)}, f32[144,128]{1,0:T(8,128)S(1)}, u32[]{:S(2)}, u32[]{:S(2)}) collective-permute-start(f32[144,128]{1,0:T(8,128)} %get-tuple-element.19), channel_id=1, source_target_pairs={{0,1},{1,2},{2,3},{4,5},{5,6},{6,7},{8,9},{9,10},{10,11},{12,13},{... | collective-permute-start | bytes 221192 | tf_op jit(solution)/shard_map/ppermute | solution.py:580
  6.4 5.3 %collective-permute-start.1 = (f32[144,128]{1,0:T(8,128)}, f32[144,128]{1,0:T(8,128)S(1)}, u32[]{:S(2)}, u32[]{:S(2)}) collective-permute-start(f32[144,128]{1,0:T(8,128)} %get-tuple-element.20), channel_id=1, source_target_pairs={{1,0},{2,1},{3,2},{5,4},{6,5},{7,6},{9,8},{10,9},{11,10},{13,12},{... | collective-permute-start | bytes 221192 | tf_op jit(solution)/shard_map/ppermute | solution.py:581
  10.7 13.4 %copy-start = (f32[144,128]{1,0:T(8,128)}, f32[144,128]{1,0:T(8,128)S(1)}, u32[]{:S(2)}) copy-start(f32[144,128]{1,0:T(8,128)S(1)} %collective-permute-done.from_left) | copy-start | bytes 221188
  11.7 12.4 %copy-start.1 = (f32[144,128]{1,0:T(8,128)}, f32[144,128]{1,0:T(8,128)S(1)}, u32[]{:S(2)}) copy-start(f32[144,128]{1,0:T(8,128)S(1)} %collective-permute-done.1.from_right) | copy-start | bytes 221188
  11.7 0.8 copy-start.3
  12.5 0.8 copy-start.4
  13.4 7.0 %collective-permute-start.2 = (f32[8,1920]{1,0:T(8,128)S(1)}, f32[8,1920]{1,0:T(8,128)S(1)}, u32[]{:S(2)}, u32[]{:S(2)}) collective-permute-start(f32[8,1920]{1,0:T(8,128)S(1)} %get-tuple-element.23), channel_id=1, source_target_pairs={{0,4},{4,8},{8,12},{12,16},{16,20},{20,24},{24,28},{28,32},{32,36}... | collective-permute-start | bytes 184328 | tf_op jit(solution)/shard_map/ppermute | solution.py:580
  18.5 5.5 %collective-permute-start.3 = (f32[8,1920]{1,0:T(8,128)S(1)}, f32[8,1920]{1,0:T(8,128)S(1)}, u32[]{:S(2)}, u32[]{:S(2)}) collective-permute-start(f32[8,1920]{1,0:T(8,128)S(1)} %get-tuple-element.24), channel_id=1, source_target_pairs={{4,0},{8,4},{12,8},{16,12},{20,16},{24,20},{28,24},{32,28},{36,32}... | collective-permute-start | bytes 184328 | tf_op jit(solution)/shard_map/ppermute | solution.py:581
  20.5 3.6 %copy-start.5 = (f32[8,1920]{1,0:T(8,128)}, f32[8,1920]{1,0:T(8,128)S(1)}, u32[]{:S(2)}) copy-start(f32[8,1920]{1,0:T(8,128)S(1)} %collective-permute-done.2.above) | copy-start | bytes 184324
  24.1 0.6 copy-start.6
  89.2 23.3 %copy-start.2 = (s32[48,12]{0,1:T(8,128)S(1)}, s32[48,12]{0,1:T(8,128)}, u32[]{:S(2)}) copy-start(s32[48,12]{0,1:T(8,128)} %param.12) | copy-start | bytes 6916
  89.2 23.3 %all-to-all-start.1 = ((f32[128,16,128]{2,1,0:T(8,128)}), f32[128,16,128]{2,1,0:T(8,128)S(1)}, u32[]{:S(2)}, u32[]{:S(2)}) async-start(f32[128,16,128]{2,1,0:T(8,128)} %bitcast.14), calls=%async_computation.1 | async-start | bytes 2097152 | tf_op jit(solution)/shard_map/all_to_all | solution.py:586

commit v3 on v2

--- a/solution.py
+++ b/solution.py
@@ -18,9 +18,9 @@
 COLS = TILES * LANES
 WIDE = (TILES + 3) * LANES
 OWN = 2 * LANES
-SEND = 32
-BACK = 16
-AGE_ROW = 14
+SEND = 2 * CAP + 1
+BACK = CAP
+AGE_ROW = 2 * CAP
 
 D0 = 0.05 + 0.95 / (1.0 + 5.0**16)
 
@@ -75,14 +75,29 @@
     return copies
 
 
-def pack_y_kernel(u, h, a, to_left, to_right, left, right, sems):
+Z_SHIFTS = ((0, (0, 3, 6)), (ROWS - 8, (3, 6, 0)))
+
+
+def three_fields(fields, shifts):
+    u, h, a = [pltpu.roll(v, s, 0) if s else v for v, s in zip(fields, shifts)]
+    row = lax.broadcasted_iota(jnp.int32, u.shape, 0)
+    return jnp.where(row < 3, u, jnp.where(row < 6, h, a))
+
+
+def pack_y_kernel(u, h, a, to_left, to_right, up, down, left, right, ends, sems):
     wide = 2 * LANES
     pairs = []
     for f, field in enumerate((u, h, a)):
         pairs.append((field.at[:, 0:wide], left.at[f]))
         pairs.append((field.at[:, COLS - wide : COLS], right.at[f]))
+        pairs.append((field.at[0:8, :], ends.at[0, f]))
+        pairs.append((field.at[ROWS - 8 : ROWS, :], ends.at[1, f]))
     for copy in start_all(pairs, sems):
         copy.wait()
+    for out, e, (_, shifts) in zip((up, down), (0, 1), Z_SHIFTS):
+        zero = jnp.zeros((8, LANES), F32)
+        out[:, 0:LANES], out[:, LANES:OWN], out[:, OWN + COLS : WIDE] = zero, zero, zero
+        out[:, OWN : OWN + COLS] = three_fields([ends[e, f] for f in range(3)], shifts)
     lane = lanes_of((ROWS, LANES))
     first, second = slice(0, LANES), slice(LANES, wide)
     to_left[0:ROWS, :] = left[0, :, first]
@@ -103,17 +118,19 @@
 
 def pack_y(u, h, a):
     shape = jax.ShapeDtypeStruct((3 * ROWS, LANES), F32)
+    rows = jax.ShapeDtypeStruct((8, WIDE), F32)
     return pl.pallas_call(
         pack_y_kernel,
-        out_shape=(shape, shape),
+        out_shape=(shape, shape, rows, rows),
         in_specs=[HBM] * 3,
-        out_specs=(VMEM, VMEM),
+        out_specs=[VMEM] * 4,
         scratch_shapes=[
             pltpu.VMEM((3, ROWS, 2 * LANES), F32),
             pltpu.VMEM((3, ROWS, 2 * LANES), F32),
-            pltpu.SemaphoreType.DMA((6,)),
+            pltpu.VMEM((2, 3, 8, COLS), F32),
+            pltpu.SemaphoreType.DMA((12,)),
         ],
-        compiler_params=whole_grant(288 * 2**10),
+        compiler_params=whole_grant(500 * 2**10),
     )(u, h, a)
 
 
@@ -137,21 +154,16 @@
     )
 
 
-Z_SHIFTS = (("up", 0, (0, 3, 6)), ("down", ROWS - 8, (3, 6, 0)))
-
-
-def three_fields(fields, shifts):
-    u, h, a = [pltpu.roll(v, s, 0) if s else v for v, s in zip(fields, shifts)]
-    row = lax.broadcasted_iota(jnp.int32, u.shape, 0)
-    return jnp.where(row < 3, u, jnp.where(row < 6, h, a))
-
-
-def pack_z_kernel(up_own, down_own, from_left, from_right, up, down):
-    for out, own, (_, lo, shifts) in zip((up, down), (up_own, down_own), Z_SHIFTS):
+def pack_z_kernel(up_own, down_own, from_left, from_right, up, down, edges, sems):
+    pairs = []
+    for e, (out, (lo, shifts)) in enumerate(zip((up, down), Z_SHIFTS)):
         sides = side_tiles(from_left, from_right, lo, 8)
-        out[:, OWN : OWN + COLS] = own[...]
-        for t, at in enumerate((0, LANES, OWN + COLS)):
-            out[:, at : at + LANES] = three_fields([side[t] for side in sides], shifts)
+        for t in range(3):
+            edges[e, :, t * LANES : (t + 1) * LANES] = three_fields([side[t] for side in sides], shifts)
+        pairs.append((edges.at[e, :, 0:OWN], out.at[:, 0:OWN]))
+        pairs.append((edges.at[e, :, OWN : 3 * LANES], out.at[:, OWN + COLS : WIDE]))
+    for copy in start_all(pairs, sems):
+        copy.wait()
 
 
 def pack_z(up_own, down_own, from_left, from_right):
@@ -159,22 +171,20 @@
     return pl.pallas_call(
         pack_z_kernel,
         out_shape=(shape, shape),
-        in_specs=[VMEM] * 4,
-        out_specs=(VMEM, VMEM),
-        compiler_params=grant(4),
+        in_specs=[HBM, HBM, VMEM, VMEM],
+        out_specs=(HBM, HBM),
+        input_output_aliases={0: 0, 1: 1},
+        scratch_shapes=[pltpu.VMEM((2, 8, 3 * LANES), F32), pltpu.SemaphoreType.DMA((4,))],
+        compiler_params=whole_grant(200 * 2**10),
     )(up_own, down_own, from_left, from_right)
 
 
-def prepare_kernel(place, times, keeper, u, h, a, table, up, down, ends, sems):
-    pairs = []
-    for f, field in enumerate((u, h, a)):
-        pairs.append((field.at[0:8, :], ends.at[0, f]))
-        pairs.append((field.at[ROWS - 8 : ROWS, :], ends.at[1, f]))
-    copies = start_all(pairs, sems)
+def table_kernel(times, keeper, table):
+    first = lax.axis_index("gz") * (ROWS // LIFT)
     lane = lanes_of((ROWS, LANES))
     solid = []
     for r in range(ROWS // LIFT):
-        age = 2400.0 - jnp.full((LIFT, LANES), times[place[0] * (ROWS // LIFT) + r], jnp.int32).astype(F32)
+        age = 2400.0 - jnp.full((LIFT, LANES), times[first + r], jnp.int32).astype(F32)
         solid.append(jnp.sqrt(600.0 / age) + 0.2)
     solid = jnp.concatenate(solid, axis=0)
     owners, slots = [], []
@@ -190,36 +200,29 @@
         precision=lax.Precision.HIGHEST,
         preferred_element_type=F32,
     )
-    for copy in copies:
-        copy.wait()
-    for out, e, (_, _, shifts) in zip((up, down), (0, 1), Z_SHIFTS):
-        out[...] = three_fields([ends[e, f] for f in range(3)], shifts)
-
-
-def prepare(place, times, keeper, u, h, a):
-    rows = jax.ShapeDtypeStruct((8, COLS), F32)
+
+
+def solid_table(times, keeper):
     return pl.pallas_call(
-        prepare_kernel,
-        out_shape=(jax.ShapeDtypeStruct((LANES, LANES), F32), rows, rows),
-        in_specs=[SMEM, SMEM, VMEM] + [HBM] * 3,
-        out_specs=[VMEM] * 3,
-        scratch_shapes=[pltpu.VMEM((2, 3, 8, COLS), F32), pltpu.SemaphoreType.DMA((6,))],
-        compiler_params=whole_grant(544 * 2**10),
-    )(place, times, keeper, u, h, a)
+        table_kernel,
+        out_shape=jax.ShapeDtypeStruct((LANES, LANES), F32),
+        in_specs=[SMEM, VMEM],
+        out_specs=VMEM,
+        compiler_params=whole_grant(600 * 2**10),
+    )(times, keeper)
 
 
 def sweep_kernel(
-    place,
     keeper,
     tally,
     u_in,
     h_in,
     a_in,
-    from_left,
-    from_right,
-    above,
-    below,
-    table,
+    left_hbm,
+    right_hbm,
+    above_hbm,
+    below_hbm,
+    table_hbm,
     t_hbm,
     h_hbm,
     m_hbm,
@@ -235,18 +238,26 @@
     h_out,
     m_out,
     send,
+    from_left,
+    from_right,
+    above,
+    below,
+    table,
     sems,
 ):
-    gz, gy, last_z, last_y = place[0], place[1], place[2], place[3]
+    gz, gy = lax.axis_index("gz"), lax.axis_index("gy")
+    last_z, last_y = lax.axis_size("gz") - 1, lax.axis_size("gy") - 1
     tiles = ROWS // 8 + 1
 
     own_cells = (slice(0, ROWS), slice(OWN, OWN + COLS))
-    loads = start_all(
-        [(src, wide.at[own_cells]) for src, wide in ((u_in, u_first), (h_in, h_first), (a_in, a_wide))],
-        sems,
-    )
+    pairs = [(src, wide.at[own_cells]) for src, wide in ((u_in, u_first), (h_in, h_first), (a_in, a_wide))]
+    pairs += [(left_hbm, from_left), (right_hbm, from_right), (above_hbm, above), (below_hbm, below)]
+    pairs += [(table_hbm, table)]
+    loads = start_all(pairs, sems)
 
     send[...] = jnp.zeros_like(send)
+    for copy in loads:
+        copy.wait()
     for o in range(LANES):
         send[o * SEND + AGE_ROW : o * SEND + AGE_ROW + 1, :] = table[o : o + 1, :]
 
@@ -272,21 +283,14 @@
     above_is, below_is = (gz > 0).astype(jnp.int32), (gz < last_z).astype(jnp.int32)
     inside_columns = jnp.where(on_own, 1, jnp.where(on_left, left_is, right_is))
 
-    def derived(h):
-        d = excess_diffusivity(h)
-        return d, d * h
-
-    for copy in loads:
-        copy.wait()
-
     def fill(r, carry):
         rows = pl.ds(pl.multiple_of(r * 8, 8), 8)
         h = h_first[rows, :]
-        d, dh = derived(h)
         fields[0, 0, rows, :] = u_first[rows, :]
         fields[0, 1, rows, :] = h
-        fields[0, 2, rows, :] = d
-        fields[0, 3, rows, :] = dh
+        fields[0, 2, rows, :] = excess_diffusivity(h)
+        for f in range(3):
+            fields[1, f, rows, 0:LANES] = jnp.zeros((8, LANES), F32)
         return carry
 
     lax.fori_loop(0, tiles, fill, 0)
@@ -299,19 +303,21 @@
         def around(f):
             v = fields[src, f, here, :]
             lower, upper = fields[src, f, before, :], fields[src, f, after, :]
-            total = pltpu.roll(jnp.where(row8 == 0, upper, v), 7, 0)
-            total = total + pltpu.roll(jnp.where(row8 == 7, lower, v), 1, 0)
-            total = total + pltpu.roll(v, WIDE - NX, 1)
-            total = total + pltpu.roll(v, NX, 1)
-            total = total + pltpu.roll(jnp.where(not_first, v, 0.0), WIDE - 1, 1)
-            total = total + pltpu.roll(jnp.where(not_last, v, 0.0), 1, 1)
-            return total
+            return (
+                pltpu.roll(jnp.where(row8 == 0, upper, v), 7, 0),
+                pltpu.roll(jnp.where(row8 == 7, lower, v), 1, 0),
+                pltpu.roll(v, WIDE - NX, 1),
+                pltpu.roll(v, NX, 1),
+                pltpu.roll(jnp.where(not_first, v, 0.0), WIDE - 1, 1),
+                pltpu.roll(jnp.where(not_last, v, 0.0), 1, 1),
+            )
 
         u, h, d = fields[src, 0, here, :], fields[src, 1, here, :], fields[src, 2, here, :]
         r_now = rate_of(u, h, a_wide[here, :])
-        u_next = (u_first[here, :] + 4.0 * r_now + around(0)) * (1.0 / 7.0)
-        conduct = 3.0 * (d + 2.0 * D0) + 0.5 * around(2)
-        inflow = 0.5 * ((d + 2.0 * D0) * around(1) + around(3))
+        u_next = (u_first[here, :] + 4.0 * r_now + sum(around(0))) * (1.0 / 7.0)
+        hs, ds = around(1), around(2)
+        conduct = 3.0 * (d + 2.0 * D0) + 0.5 * sum(ds)
+        inflow = 0.5 * ((d + 2.0 * D0) * sum(hs) + sum(x * y for x, y in zip(ds, hs)))
         h_next = (h_first[here, :] - 0.5 * r_now + inflow) / (1.0 + conduct)
         return u_next, h_next
 
@@ -323,11 +329,9 @@
             below_in, above_in = jnp.maximum(own_rows, below_is), jnp.maximum(own_rows, above_is)
             keep = inside_columns * jnp.where(row8 < 4, below_in, above_in) > 0
             u, h = jnp.where(keep, u, 0.0), jnp.where(keep, h, 0.0)
-            d, dh = derived(h)
-            fields[1 - src, 0, rows, :] = u
-            fields[1 - src, 1, rows, :] = h
-            fields[1 - src, 2, rows, :] = d
-            fields[1 - src, 3, rows, :] = dh
+            d = excess_diffusivity(h)
+            for f, v in enumerate((u, h, d)):
+                fields[1 - src, f, rows, LANES:WIDE] = v[:, LANES:WIDE]
             return carry
 
         lax.fori_loop(0, tiles, run, 0)
@@ -370,7 +374,7 @@
             at = place_of(keeper[j, z], SEND)
             block = pl.ds(j * ROWS + z, 1)
             send[pl.ds(at, 1), :] = phi_buf[block, :]
-            send[pl.ds(at + 16, 1), :] = load_buf[block, :]
+            send[pl.ds(at + CAP, 1), :] = load_buf[block, :]
         return carry
 
     lax.fori_loop(0, ROWS, scatter, 0)
@@ -381,19 +385,19 @@
     message.wait()
 
 
-def sweeps(place, keeper, tally, u, h, a, from_left, from_right, above, below, table):
+def sweeps(keeper, tally, u, h, a, from_left, from_right, above, below, table):
     grid_shape = jax.ShapeDtypeStruct((ROWS, COLS), F32)
     wide = pltpu.VMEM((ROWS + 8, WIDE), F32)
     return pl.pallas_call(
         sweep_kernel,
         out_shape=(grid_shape, grid_shape, grid_shape, jax.ShapeDtypeStruct((LANES * SEND, LANES), F32)),
-        in_specs=[SMEM, SMEM, VMEM] + [HBM] * 3 + [VMEM] * 5,
+        in_specs=[SMEM, VMEM] + [HBM] * 8,
         out_specs=[HBM] * 4,
         scratch_shapes=[
             wide,
             wide,
             wide,
-            pltpu.VMEM((2, 4, ROWS + 8, WIDE), F32),
+            pltpu.VMEM((2, 3, ROWS + 8, WIDE), F32),
             pltpu.VMEM((TILES * ROWS, LANES), F32),
             pltpu.VMEM((TILES * ROWS, LANES), F32),
             pltpu.VMEM((ROWS, LANES), jnp.int32),
@@ -401,13 +405,20 @@
             pltpu.VMEM((ROWS, COLS), F32),
             pltpu.VMEM((ROWS, COLS), F32),
             pltpu.VMEM((LANES * SEND, LANES), F32),
-            pltpu.SemaphoreType.DMA((4,)),
+            pltpu.VMEM((3 * ROWS, LANES), F32),
+            pltpu.VMEM((3 * ROWS, LANES), F32),
+            pltpu.VMEM((8, WIDE), F32),
+            pltpu.VMEM((8, WIDE), F32),
+            pltpu.VMEM((LANES, LANES), F32),
+            pltpu.SemaphoreType.DMA((8,)),
         ],
-        compiler_params=whole_grant(544 * 2**10),
-    )(place, keeper, tally, u, h, a, from_left, from_right, above, below, table)
+        compiler_params=whole_grant(400 * 2**10),
+    )(keeper, tally, u, h, a, from_left, from_right, above, below, table)
 
 
 GROUP = 16
+PAD = 16
+UNROLL = 4
 PARTS = LANES // GROUP
 
 
@@ -421,7 +432,7 @@
 
 def unit_change(prior, got, at, scale):
     phi = jnp.broadcast_to(got[pl.ds(at, 1), :], (UNITS, LANES))
-    load = jnp.broadcast_to(got[pl.ds(at + 16, 1), :], (UNITS, LANES))
+    load = jnp.broadcast_to(got[pl.ds(at + CAP, 1), :], (UNITS, LANES))
     return (1.0 - jnp.exp2(phi * scale)) * (load - prior)
 
 
@@ -445,39 +456,43 @@
     return pairs[0]
 
 
-def load_states(chain_hbm, tension_hbm, chain, tension, sems):
-    n = GROUP * CAP
+def load_states(got_hbm, chain_hbm, tension_hbm, got, chain, tension, sems):
     pairs = [(tension_hbm, tension.at[0 : LANES * CAP])]
-    pairs += [(chain_hbm.at[i * n : (i + 1) * n], chain.at[i * n : (i + 1) * n]) for i in range(PARTS)]
+    for i in range(PARTS):
+        for rows, src, dst in ((GROUP * SEND, got_hbm, got), (GROUP * CAP, chain_hbm, chain)):
+            part = slice(i * rows, (i + 1) * rows)
+            pairs.append((src.at[part], dst.at[part]))
     return start_all(pairs, sems)
 
 
-def creep_kernel(got, chain_hbm, tension_hbm, creep_hbm, chain, tension, creep, in_sems, out_sems):
-    loads = load_states(chain_hbm, tension_hbm, chain, tension, in_sems)
+def creep_kernel(got_hbm, chain_hbm, tension_hbm, creep_hbm, got, chain, tension, creep, in_sems, out_sems):
+    tension[LANES * CAP :, :] = jnp.ones((PAD, LANES), F32)
+    loads = load_states(got_hbm, chain_hbm, tension_hbm, got, chain, tension, in_sems)
     scale = decay_rates()
-    diagonal = lanes_of((BACK, LANES)) == lax.broadcasted_iota(jnp.int32, (BACK, LANES), 0)
+    diagonal = lanes_of((16, LANES)) == lax.broadcasted_iota(jnp.int32, (16, LANES), 0)
 
     def one(s, carry):
-        base = pl.multiple_of(s * SEND, SEND)
-        ages = jnp.broadcast_to(got[pl.ds(base + AGE_ROW, 1), :], (BACK, LANES))
+        base = s * SEND
+        ages = jnp.broadcast_to(got[pl.ds(base + AGE_ROW, 1), :], (16, LANES))
         solid = jnp.sum(jnp.where(diagonal, ages, 0.0), axis=1, keepdims=True)
         zero = jnp.zeros((UNITS, LANES), F32)
         changes = [unit_change(chain[s * CAP + k], got, base + k, scale) for k in range(CAP)]
-        changes += [zero] * (BACK - CAP)
+        changes += [zero] * (16 - CAP)
         total = jnp.concatenate([sum_units(changes[:8]), sum_units(changes[8:])], axis=0)
-        rows = pl.ds(pl.multiple_of(s * BACK, BACK), BACK)
-        phi, load = got[pl.ds(base, 16), :], got[pl.ds(base + 16, 16), :]
-        before = tension[pl.ds(s * CAP, BACK), :]
+        rows = pl.ds(s * CAP, 16)
+        phi, load = got[pl.ds(base, 16), :], got[pl.ds(base + CAP - 1, 16), :]
+        load = pltpu.roll(load, 15, 0)
+        before = tension[rows, :]
         after = before / (1.0 + 0.2 * phi * before)
         creep[rows, :] = solid * total + (0.1 / 0.15) * phi * after * load
         return carry
 
-    tension[LANES * CAP :, :] = jnp.ones((BACK, LANES), F32)
     loads[0].wait()
     stores = []
     for i in range(PARTS):
-        loads[1 + i].wait()
-        lax.fori_loop(i * GROUP, (i + 1) * GROUP, one, 0, unroll=2)
+        for copy in loads[1 + 2 * i : 3 + 2 * i]:
+            copy.wait()
+        lax.fori_loop(i * GROUP, (i + 1) * GROUP, one, 0, unroll=UNROLL)
         part = slice(i * GROUP * BACK, (i + 1) * GROUP * BACK)
         stores.append(pltpu.make_async_copy(creep.at[part], creep_hbm.at[part], out_sems.at[i]))
         stores[-1].start()
@@ -485,29 +500,32 @@
         copy.wait()
 
 
-def state_kernel(got, chain_hbm, tension_hbm, chain_new, tension_new, chain, tension, in_sems, out_sems):
-    loads = load_states(chain_hbm, tension_hbm, chain, tension, in_sems)
+def state_kernel(
+    got_hbm, chain_hbm, tension_hbm, chain_new, tension_new, got, chain, tension, in_sems, out_sems
+):
+    tension[LANES * CAP :, :] = jnp.ones((PAD, LANES), F32)
+    loads = load_states(got_hbm, chain_hbm, tension_hbm, got, chain, tension, in_sems)
     scale = decay_rates()
-    used = lax.broadcasted_iota(jnp.int32, (BACK, LANES), 0) < CAP
+    used = lax.broadcasted_iota(jnp.int32, (16, LANES), 0) < CAP
 
     def one(s, carry):
-        base = pl.multiple_of(s * SEND, SEND)
+        base = s * SEND
         for k in range(CAP):
             prior = chain[s * CAP + k]
             chain[s * CAP + k] = prior + unit_change(prior, got, base + k, scale)
         phi = got[pl.ds(base, 16), :]
-        rows = pl.ds(s * CAP, BACK)
+        rows = pl.ds(s * CAP, 16)
         before = tension[rows, :]
         tension[rows, :] = jnp.where(used, before / (1.0 + 0.2 * phi * before), before)
         return carry
 
-    tension[LANES * CAP :, :] = jnp.ones((BACK, LANES), F32)
     loads[0].wait()
     stores = []
     n = GROUP * CAP
     for i in range(PARTS):
-        loads[1 + i].wait()
-        lax.fori_loop(i * GROUP, (i + 1) * GROUP, one, 0)
+        for copy in loads[1 + 2 * i : 3 + 2 * i]:
+            copy.wait()
+        lax.fori_loop(i * GROUP, (i + 1) * GROUP, one, 0, unroll=2)
         part = slice(i * n, (i + 1) * n)
         stores.append(pltpu.make_async_copy(chain.at[part], chain_new.at[part], out_sems.at[i]))
         stores[-1].start()
@@ -519,10 +537,11 @@
 
 def owner_scratch(creep):
     return [
+        pltpu.VMEM((LANES * SEND, LANES), F32),
         pltpu.VMEM((LANES * CAP, UNITS, LANES), F32),
-        pltpu.VMEM((LANES * CAP + BACK, LANES), F32),
+        pltpu.VMEM((LANES * CAP + PAD, LANES), F32),
         *creep,
-        pltpu.SemaphoreType.DMA((PARTS + 1,)),
+        pltpu.SemaphoreType.DMA((2 * PARTS + 1,)),
         pltpu.SemaphoreType.DMA((PARTS + 1,)),
     ]
 
@@ -532,10 +551,10 @@
     return pl.pallas_call(
         creep_kernel,
         out_shape=jax.ShapeDtypeStruct(shape, F32),
-        in_specs=[VMEM, HBM, HBM],
+        in_specs=[HBM] * 3,
         out_specs=HBM,
-        scratch_shapes=owner_scratch([pltpu.VMEM(shape, F32)]),
-        compiler_params=whole_grant(2560 * 2**10),
+        scratch_shapes=owner_scratch([pltpu.VMEM((LANES * CAP + PAD, LANES), F32)]),
+        compiler_params=whole_grant(600 * 2**10),
         cost_estimate=pl.CostEstimate(flops=20 * chain.size, bytes_accessed=4 * chain.size, transcendentals=chain.size),
     )(got, chain, tension)
 
@@ -544,10 +563,10 @@
     return pl.pallas_call(
         state_kernel,
         out_shape=(jax.ShapeDtypeStruct(chain.shape, F32), jax.ShapeDtypeStruct(tension.shape, F32)),
-        in_specs=[VMEM, HBM, HBM],
+        in_specs=[HBM] * 3,
         out_specs=(HBM, HBM),
         scratch_shapes=owner_scratch([]),
-        compiler_params=whole_grant(2560 * 2**10),
+        compiler_params=whole_grant(600 * 2**10),
         cost_estimate=pl.CostEstimate(flops=20 * chain.size, bytes_accessed=8 * chain.size, transcendentals=chain.size),
     )(got, chain, tension)
 
@@ -583,19 +602,19 @@
 
 
 def exchange(x):
-    return lax.all_to_all(x, ("gz", "gy"), split_axis=0, concat_axis=0, tiled=True)
+    flat = x.reshape(LANES, 1, -1)
+    return lax.all_to_all(flat, ("gz", "gy"), split_axis=0, concat_axis=0, tiled=True).reshape(x.shape)
 
 
 def body(u, h, a, tally, keeper, times, chain, tension):
-    ends = [jnp.int32(lax.axis_size(n) - 1) for n in ("gz", "gy")]
-    place = jnp.stack([lax.axis_index("gz"), lax.axis_index("gy"), *ends]).astype(jnp.int32)
     tally, keeper = tally.T, keeper.T
-    to_left, to_right = pack_y(u, h, a)
+    to_left, to_right, up_own, down_own = pack_y(u, h, a)
     from_left, from_right = both_ways("gy", to_left, to_right)
-    table, up_own, down_own = prepare(place, times, keeper, u, h, a)
+    table = solid_table(times, keeper)
+    up_own, down_own, table = lax.optimization_barrier((up_own, down_own, table))
     up, down = pack_z(up_own, down_own, from_left, from_right)
     above, below = both_ways("gz", up, down)
-    t_new, h_new, m_new, send = sweeps(place, keeper, tally, u, h, a, from_left, from_right, above, below, table)
+    t_new, h_new, m_new, send = sweeps(keeper, tally, u, h, a, from_left, from_right, above, below, table)
     got = exchange(send)
     creep = creep_of(got, chain, tension)
     back = exchange(creep)

time: 116 us -> 109 us (0.940)
  Pallas kernels: 37.4 us -> 33.1 us
  blocking collectives: 42.2 us -> 40.1 us
  local copies, waits for them, and re-layouts: 2.25 us -> 0.63 us
    pallas_call x1, Pallas kernels: 9.17 us -> 5.64 us  [creep_of(): pl.pallas_call(creep_kernel, out_shape=jax.ShapeDtypeStruct(shape, F32),...]
    all_to_all x1, blocking collectives: 42.2 us -> 40.1 us  [exchange(): lax.all_to_all(flat, ('gz', 'gy'), split_axis=0, concat_axis=0, tiled=True)]
    unnamed x14 -> x8, local copies, waits for them, and re-layouts: 2.25 us -> 0.63 us
    pallas_call x3, Pallas kernels: 4.12 us -> 5.61 us  [the longest x1 2.04 us: solid_table(): pl.pallas_call(table_kernel, out_shape=jax.ShapeDtypeStruct((LANES, LANES...]
    pallas_call x1, Pallas kernels: 13.1 us -> 11.7 us  [sweeps(): pl.pallas_call(sweep_kernel, out_shape=(grid_shape, grid_shape, grid_shap...]
    ppermute x2, waiting for transfers between devices: 4.62 us -> 5.87 us  [both_ways(): lax.ppermute(to_lower, axis, [(i + 1, i) for i in range(ends)])]
  transfers between devices with their start and end apart: 5 -> 5, of which waited for: 3 -> 3; matrix products, arithmetic and copies ran while one was open for 1% -> 0% of each run, Pallas kernels for 9% -> 9%
where the time goes in v3:
time: 109 us; the launch traced here: 108 us
  blocking collectives  40.1 us (37%)
  Pallas kernels  33.1 us (30%)
  starting transfers between devices  17.1 us (16%)
  waiting for transfers between devices  16.4 us (15%)
    all_to_all x1, blocking collectives, exchange(): lax.all_to_all(flat, ('gz', 'gy'), split_axis=0, concat_axis=0, tiled=True)  40.1 us
    pallas_call x1, Pallas kernels, sweeps(): pl.pallas_call(sweep_kernel, out_shape=(grid_shape, grid_shape, grid_shap...  11.7 us
    all_to_all x1, waiting for transfers between devices, exchange(): lax.all_to_all(flat, ('gz', 'gy'), split_axis=0, concat_axis=0, tiled=True)  10.5 us
    ppermute x2, starting transfers between devices, both_ways(): lax.ppermute(to_higher, axis, [(i, i + 1) for i in range(ends)])  9.14 us
    pallas_call x1, Pallas kernels, states_of(): pl.pallas_call(state_kernel, out_shape=(jax.ShapeDtypeStruct(chain.shape,...  7.33 us
    ppermute x2, waiting for transfers between devices, both_ways(): lax.ppermute(to_lower, axis, [(i + 1, i) for i in range(ends)])  5.87 us
    pallas_call x1, Pallas kernels, creep_of(): pl.pallas_call(creep_kernel, out_shape=jax.ShapeDtypeStruct(shape, F32),...  5.64 us
    all_to_all x1, starting transfers between devices, exchange(): lax.all_to_all(flat, ('gz', 'gy'), split_axis=0, concat_axis=0, tiled=True)  4.77 us
  transfers between devices with their start and end apart: 5, of which 3 were waited for; matrix products, arithmetic and copies ran while one was open for 0% of the time, Pallas kernels for 9%

profile of v3, /device:TPU:1, one launch (start us, length us, event | category | flops | bytes accessed | tf_op | source)
XLA Modules:
  0.0 108.1 jit_solution(7726186187224586613)
XLA Ops:
  0.6 1.9 %shard_map.127 = (f32[144,128]{1,0:T(8,128)}, f32[144,128]{1,0:T(8,128)}, f32[8,1920]{1,0:T(8,128)}, f32[8,1920]{1,0:T(8,128)}) custom-call(f32[48,1536]{1,0:T(8,128)} %u_in.1, f32[48,1536]{1,0:T(8,128)} %h_in.1, f32[48,1536]{1,0:T(8,128)} %a_in.1), custom_call_target="tpu_custom_call" | custom-call | tf_op jit(solution)/shard_map/pallas_call | solution.py:122
  2.6 4.0 %collective-permute-start = (f32[144,128]{1,0:T(8,128)}, f32[144,128]{1,0:T(8,128)S(1)}, u32[]{:S(2)}, u32[]{:S(2)}) collective-permute-start(f32[144,128]{1,0:T(8,128)} %get-tuple-element.21), channel_id=1, source_target_pairs={{0,1},{1,2},{2,3},{4,5},{5,6},{6,7},{8,9},{9,10},{10,11},{12,13},{... | collective-permute-start | bytes 221192 | tf_op jit(solution)/shard_map/ppermute | solution.py:599
  6.6 1.3 %collective-permute-start.1 = (f32[144,128]{1,0:T(8,128)}, f32[144,128]{1,0:T(8,128)}, u32[]{:S(2)}, u32[]{:S(2)}) collective-permute-start(f32[144,128]{1,0:T(8,128)} %get-tuple-element.22), channel_id=1, source_target_pairs={{1,0},{2,1},{3,2},{5,4},{6,5},{7,6},{9,8},{10,9},{11,10},{13,12},{... | collective-permute-start | bytes 221192 | tf_op jit(solution)/shard_map/ppermute | solution.py:600
  7.9 2.0 %shard_map.128.table_hbm = f32[128,128]{1,0:T(8,128)} custom-call(s32[192]{0:T(256)} %times.1, s32[12,48]{1,0:T(8,128)} %bitcast.6), custom_call_target="tpu_custom_call" | custom-call | tf_op jit(solution)/shard_map/pallas_call | solution.py:206
  10.0 0.0 collective-permute-done.from_left.left_hbm
  10.0 0.0 copy-start.1
  10.0 2.1 %collective-permute-done.1.from_right.right_hbm = f32[144,128]{1,0:T(8,128)} collective-permute-done((f32[144,128]{1,0:T(8,128)}, f32[144,128]{1,0:T(8,128)}, u32[]{:S(2)}, u32[]{:S(2)}) %collective-permute-start.1) | collective-permute-done | bytes 73760 | tf_op jit(solution)/shard_map/ppermute | solution.py:600
  12.0 0.0 copy-done.1
  12.0 1.6 %shard_map.129 = (f32[8,1920]{1,0:T(8,128)}, f32[8,1920]{1,0:T(8,128)}) custom-call(f32[8,1920]{1,0:T(8,128)} %get-tuple-element.25.up_own, f32[8,1920]{1,0:T(8,128)} %get-tuple-element.26.down_own, f32[144,128]{1,0:T(8,128)} %copy-done.1, f32[144,128]{1,0:T(8,128)} %collective-permute-done.1.from_right.right_hbm), custom_call_target="tpu_custom_call", output_to_operand_aliasing={{0}: (0, {}), {1}: (1, {})} | custom-call | tf_op jit(solution)/shard_map/pallas_call | solution.py:171
  13.7 5.1 %collective-permute-start.2 = (f32[8,1920]{1,0:T(8,128)}, f32[8,1920]{1,0:T(8,128)S(1)}, u32[]{:S(2)}, u32[]{:S(2)}) collective-permute-start(f32[8,1920]{1,0:T(8,128)} %get-tuple-element.27), channel_id=1, source_target_pairs={{0,4},{4,8},{8,12},{12,16},{16,20},{20,24},{24,28},{28,32},{32,36}... | collective-permute-start | bytes 184328 | tf_op jit(solution)/shard_map/ppermute | solution.py:599
  18.8 1.9 %collective-permute-start.3 = (f32[8,1920]{1,0:T(8,128)}, f32[8,1920]{1,0:T(8,128)S(1)}, u32[]{:S(2)}, u32[]{:S(2)}) collective-permute-start(f32[8,1920]{1,0:T(8,128)} %get-tuple-element.28), channel_id=1, source_target_pairs={{4,0},{8,4},{12,8},{16,12},{20,16},{24,20},{28,24},{32,28},{36,32}... | collective-permute-start | bytes 184328 | tf_op jit(solution)/shard_map/ppermute | solution.py:600
  20.7 0.0 collective-permute-done.2.above_hbm
  20.7 0.0 copy-start.2
  20.7 3.8 %collective-permute-done.3.below_hbm = f32[8,1920]{1,0:T(8,128)S(1)} collective-permute-done((f32[8,1920]{1,0:T(8,128)}, f32[8,1920]{1,0:T(8,128)S(1)}, u32[]{:S(2)}, u32[]{:S(2)}) %collective-permute-start.3) | collective-permute-done | bytes 61472 | tf_op jit(solution)/shard_map/ppermute | solution.py:600
  24.5 0.0 copy-start.3
  24.5 0.0 copy-done.2
  24.5 0.6 copy-done.3
  25.2 11.7 %shard_map.130 = (f32[48,1536]{1,0:T(8,128)}, f32[48,1536]{1,0:T(8,128)}, f32[48,1536]{1,0:T(8,128)}, f32[3712,128]{1,0:T(8,128)}) custom-call(s32[12,48]{1,0:T(8,128)} %bitcast.7, s32[12,48]{1,0:T(8,128)} %bitcast.13, f32[48,1536]{1,0:T(8,128)} %u_in.1, f32[48,1536]{1,0:T(8,128)} %h_in.1, f32[48,1536]{1,0:T(8,128)} %a_in.1, f32[144,128]{1,0:T(8,128)} %copy-done.1, ...), custom_call_target="tpu_custom_call" | custom-call | tf_op jit(solution)/shard_map/pallas_call | solution.py:391
  36.9 40.1 %all_to_all.10 = f32[128,1,3712]{2,1,0:T(1,128)} all-to-all(f32[128,1,3712]{2,1,0:T(1,128)} %bitcast.12), channel_id=1, replica_groups=mesh['gz'=32,'gy'=4] {'gz','gy'}, dimensions={0} | all-to-all | bytes 3801088 | tf_op jit(solution)/shard_map/all_to_all | solution.py:606
  77.0 5.6 %shard_map.131 = f32[1792,128]{1,0:T(8,128)} custom-call(f32[3712,128]{1,0:T(8,128)} %bitcast.9, f32[1792,8,128]{2,1,0:T(8,128)} %chain_hbm.3, f32[1792,128]{1,0:T(8,128)} %tension_hbm.3), custom_call_target="tpu_custom_call" | custom-call | flops 36700160 | bytes 7340032 | tf_op jit(solution)/shard_map/pallas_call | solution.py:551
  82.7 0.0 copy-start
  82.7 4.8 %all-to-all-start.1 = ((f32[128,1,1792]{2,1,0:T(1,128)}), f32[128,1,1792]{2,1,0:T(1,128)}, u32[]{:S(2)}, u32[]{:S(2)}) async-start(f32[128,1,1792]{2,1,0:T(1,128)} %bitcast.11), calls=%async_computation.1 | async-start | bytes 1835008 | tf_op jit(solution)/shard_map/all_to_all | solution.py:606
  87.5 7.3 %shard_map.133 = (f32[1792,8,128]{2,1,0:T(8,128)}, f32[1792,128]{1,0:T(8,128)}) custom-call(f32[3712,128]{1,0:T(8,128)} %bitcast.10, f32[1792,8,128]{2,1,0:T(8,128)} %chain_hbm.3, f32[1792,128]{1,0:T(8,128)} %tension_hbm.3), custom_call_target="tpu_custom_call" | custom-call | flops 36700160 | bytes 14680064 | tf_op jit(solution)/shard_map/pallas_call | solution.py:563
  94.8 10.5 %all-to-all-done.1 = f32[128,1,1792]{2,1,0:T(1,128)} async-done(((f32[128,1,1792]{2,1,0:T(1,128)}), f32[128,1,1792]{2,1,0:T(1,128)}, u32[]{:S(2)}, u32[]{:S(2)}) %all-to-all-start.1) | async-done | bytes 917536 | tf_op jit(solution)/shard_map/all_to_all | solution.py:606
  105.4 0.0 copy-done
  105.4 2.8 %shard_map.132 = f32[48,1536]{1,0:T(8,128)} custom-call(s32[12,48]{1,0:T(8,128)S(1)} %bitcast.8, f32[1792,128]{1,0:T(8,128)} %bitcast.5.back), custom_call_target="tpu_custom_call" | custom-call | tf_op jit(solution)/shard_map/pallas_call | solution.py:587
Async XLA Ops:
  2.6 7.4 %collective-permute-start = (f32[144,128]{1,0:T(8,128)}, f32[144,128]{1,0:T(8,128)S(1)}, u32[]{:S(2)}, u32[]{:S(2)}) collective-permute-start(f32[144,128]{1,0:T(8,128)} %get-tuple-element.21), channel_id=1, source_target_pairs={{0,1},{1,2},{2,3},{4,5},{5,6},{6,7},{8,9},{9,10},{10,11},{12,13},{... | collective-permute-start | bytes 221192 | tf_op jit(solution)/shard_map/ppermute | solution.py:599
  6.6 5.4 %collective-permute-start.1 = (f32[144,128]{1,0:T(8,128)}, f32[144,128]{1,0:T(8,128)}, u32[]{:S(2)}, u32[]{:S(2)}) collective-permute-start(f32[144,128]{1,0:T(8,128)} %get-tuple-element.22), channel_id=1, source_target_pairs={{1,0},{2,1},{3,2},{5,4},{6,5},{7,6},{9,8},{10,9},{11,10},{13,12},{... | collective-permute-start | bytes 221192 | tf_op jit(solution)/shard_map/ppermute | solution.py:600
  10.0 2.1 %copy-start.1 = (f32[144,128]{1,0:T(8,128)}, f32[144,128]{1,0:T(8,128)S(1)}, u32[]{:S(2)}) copy-start(f32[144,128]{1,0:T(8,128)S(1)} %collective-permute-done.from_left.left_hbm) | copy-start | bytes 221188
  13.7 7.0 %collective-permute-start.2 = (f32[8,1920]{1,0:T(8,128)}, f32[8,1920]{1,0:T(8,128)S(1)}, u32[]{:S(2)}, u32[]{:S(2)}) collective-permute-start(f32[8,1920]{1,0:T(8,128)} %get-tuple-element.27), channel_id=1, source_target_pairs={{0,4},{4,8},{8,12},{12,16},{16,20},{20,24},{24,28},{28,32},{32,36}... | collective-permute-start | bytes 184328 | tf_op jit(solution)/shard_map/ppermute | solution.py:599
  18.8 5.8 %collective-permute-start.3 = (f32[8,1920]{1,0:T(8,128)}, f32[8,1920]{1,0:T(8,128)S(1)}, u32[]{:S(2)}, u32[]{:S(2)}) collective-permute-start(f32[8,1920]{1,0:T(8,128)} %get-tuple-element.28), channel_id=1, source_target_pairs={{4,0},{8,4},{12,8},{16,12},{20,16},{24,20},{28,24},{32,28},{36,32}... | collective-permute-start | bytes 184328 | tf_op jit(solution)/shard_map/ppermute | solution.py:600
  20.7 3.8 %copy-start.2 = (f32[8,1920]{1,0:T(8,128)}, f32[8,1920]{1,0:T(8,128)S(1)}, u32[]{:S(2)}) copy-start(f32[8,1920]{1,0:T(8,128)S(1)} %collective-permute-done.2.above_hbm) | copy-start | bytes 184324
  24.5 0.6 copy-start.3
  82.7 22.7 %copy-start = (s32[48,12]{0,1:T(8,128)S(1)}, s32[48,12]{0,1:T(8,128)}, u32[]{:S(2)}) copy-start(s32[48,12]{0,1:T(8,128)} %param.12) | copy-start | bytes 6916
  82.7 22.7 %all-to-all-start.1 = ((f32[128,1,1792]{2,1,0:T(1,128)}), f32[128,1,1792]{2,1,0:T(1,128)}, u32[]{:S(2)}, u32[]{:S(2)}) async-start(f32[128,1,1792]{2,1,0:T(1,128)} %bitcast.11), calls=%async_computation.1 | async-start | bytes 1835008 | tf_op jit(solution)/shard_map/all_to_all | solution.py:606

commit v4 on v3

--- a/solution.py
+++ b/solution.py
@@ -137,8 +137,11 @@
 def side_tiles(from_left, from_right, lo, n):
     lane = lanes_of((n, LANES))
     rows = [slice(f * ROWS + lo, f * ROWS + lo + n) for f in range(3)]
-    lx, rx = from_left[rows[2], :], from_right[rows[2], :]
     zero = jnp.zeros((n, LANES), F32)
+    gy = lax.axis_index("gy")
+    lefts = [jnp.where(gy > 0, from_left[r, :], zero) for r in rows]
+    rights = [jnp.where(gy < lax.axis_size("gy") - 1, from_right[r, :], zero) for r in rows]
+    lx, rx = lefts[2], rights[2]
 
     def far(left_shift, right_shift):
         return jnp.where(
@@ -148,8 +151,8 @@
         )
 
     return (
-        (far(112, 32), from_left[rows[0], :], from_right[rows[0], :]),
-        (far(96, 16), from_left[rows[1], :], from_right[rows[1], :]),
+        (far(112, 32), lefts[0], rights[0]),
+        (far(96, 16), lefts[1], rights[1]),
         (zero, jnp.where(lane >= 32, lx, zero), jnp.where(lane < 96, rx, zero)),
     )
 
@@ -268,7 +271,7 @@
         wide[0:ROWS, OWN + COLS : WIDE] = side[2]
     row8 = lax.broadcasted_iota(jnp.int32, (8, WIDE), 0)
     zero = jnp.zeros((8, WIDE), F32)
-    top, bottom = above[...], below[...]
+    top, bottom = jnp.where(gz > 0, above[...], zero), jnp.where(gz < last_z, below[...], zero)
     for wide, down_shift, up_shift in ((u_first, 0, 5), (h_first, 5, 2), (a_wide, 2, 0)):
         b = pltpu.roll(bottom, down_shift, 0) if down_shift else bottom
         t = pltpu.roll(top, up_shift, 0) if up_shift else top
@@ -293,7 +296,7 @@
             fields[1, f, rows, 0:LANES] = jnp.zeros((8, LANES), F32)
         return carry
 
-    lax.fori_loop(0, tiles, fill, 0)
+    lax.fori_loop(0, tiles, fill, 0, unroll=True)
 
     def step(src, r):
         here = pl.ds(pl.multiple_of(r * 8, 8), 8)
@@ -334,7 +337,7 @@
                 fields[1 - src, f, rows, LANES:WIDE] = v[:, LANES:WIDE]
             return carry
 
-        lax.fori_loop(0, tiles, run, 0)
+        lax.fori_loop(0, tiles, run, 0, unroll=True)
 
     middle(0)
     middle(1)
@@ -365,7 +368,7 @@
             load_buf[block_rows, :] = load[:, part]
         return carry
 
-    lax.fori_loop(0, tiles - 1, last, 0)
+    lax.fori_loop(0, tiles - 1, last, 0, unroll=True)
 
     results = start_all([(t_out, t_hbm), (h_out, h_hbm), (m_out, m_hbm)], sems)
 
@@ -578,7 +581,7 @@
             blocks[pl.ds(j * ROWS + z, 1), :] = back[pl.ds(at, 1), :]
         return carry
 
-    lax.fori_loop(0, ROWS, line, 0)
+    lax.fori_loop(0, ROWS, line, 0, unroll=4)
     for j in range(TILES):
         out[:, j * LANES : (j + 1) * LANES] = blocks[j * ROWS : (j + 1) * ROWS, :]
 
@@ -595,9 +598,9 @@
 
 
 def both_ways(axis, to_lower, to_higher):
-    ends = lax.axis_size(axis) - 1
-    from_lower = lax.ppermute(to_higher, axis, [(i, i + 1) for i in range(ends)])
-    from_higher = lax.ppermute(to_lower, axis, [(i + 1, i) for i in range(ends)])
+    count = lax.axis_size(axis)
+    from_lower = lax.ppermute(to_higher, axis, [(i, (i + 1) % count) for i in range(count)])
+    from_higher = lax.ppermute(to_lower, axis, [((i + 1) % count, i) for i in range(count)])
     return from_lower, from_higher
 
 

time: 109 us -> 98.9 us (0.907)
  starting transfers between devices: 17.1 us -> 11.2 us
  Pallas kernels: 33.1 us -> 30.8 us
  waiting for transfers between devices: 16.4 us -> 14.7 us
    ppermute x4, starting transfers between devices: 12.4 us -> 6.47 us  [the longest x2 4.95 us: both_ways(): lax.ppermute(to_higher, axis, [(i, (i + 1) % count) for i in range(count)])]
    pallas_call x1, Pallas kernels: 11.7 us -> 9.64 us  [sweeps(): pl.pallas_call(sweep_kernel, out_shape=(grid_shape, grid_shape, grid_shap...]
    ppermute x4, waiting for transfers between devices: 5.87 us -> 4.15 us  [the longest x2 2.54 us: both_ways(): lax.ppermute(to_lower, axis, [((i + 1) % count, i) for i in range(count)])]
  transfers between devices with their start and end apart: 5 -> 5, of which waited for: 3 -> 3; matrix products, arithmetic and copies ran while one was open for 0% -> 0% of each run, Pallas kernels for 9% -> 10%
where the time goes in v4:
time: 98.9 us; the launch traced here: 98.4 us
  blocking collectives  39.7 us (40%)
  Pallas kernels  30.8 us (31%)
  waiting for transfers between devices  14.7 us (15%)
  starting transfers between devices  11.2 us (11%)
  local copies, waits for them, and re-layouts  1.25 us (1%)
    all_to_all x1, blocking collectives, exchange(): lax.all_to_all(flat, ('gz', 'gy'), split_axis=0, concat_axis=0, tiled=True)  39.7 us
    all_to_all x1, waiting for transfers between devices, exchange(): lax.all_to_all(flat, ('gz', 'gy'), split_axis=0, concat_axis=0, tiled=True)  10.5 us
    pallas_call x1, Pallas kernels, sweeps(): pl.pallas_call(sweep_kernel, out_shape=(grid_shape, grid_shape, grid_shap...  9.64 us
    pallas_call x1, Pallas kernels, states_of(): pl.pallas_call(state_kernel, out_shape=(jax.ShapeDtypeStruct(chain.shape,...  7.33 us
    pallas_call x1, Pallas kernels, creep_of(): pl.pallas_call(creep_kernel, out_shape=jax.ShapeDtypeStruct(shape, F32),...  5.64 us
    ppermute x2, starting transfers between devices, both_ways(): lax.ppermute(to_higher, axis, [(i, (i + 1) % count) for i in range(count)])  4.95 us
    all_to_all x1, starting transfers between devices, exchange(): lax.all_to_all(flat, ('gz', 'gy'), split_axis=0, concat_axis=0, tiled=True)  4.77 us
    pallas_call x1, Pallas kernels, collect(): pl.pallas_call(collect_kernel, out_shape=jax.ShapeDtypeStruct((ROWS, COLS...  2.61 us
  transfers between devices with their start and end apart: 5, of which 3 were waited for; matrix products, arithmetic and copies ran while one was open for 0% of the time, Pallas kernels for 10%

profile of v4, /device:TPU:1, one launch (start us, length us, event | category | flops | bytes accessed | tf_op | source)
XLA Modules:
  0.0 98.4 jit_solution(18080918508623689428)
XLA Ops:
  0.6 1.9 %shard_map.127 = (f32[144,128]{1,0:T(8,128)}, f32[144,128]{1,0:T(8,128)}, f32[8,1920]{1,0:T(8,128)}, f32[8,1920]{1,0:T(8,128)}) custom-call(f32[48,1536]{1,0:T(8,128)} %u_in.1, f32[48,1536]{1,0:T(8,128)} %h_in.1, f32[48,1536]{1,0:T(8,128)} %a_in.1), custom_call_target="tpu_custom_call" | custom-call | tf_op jit(solution)/shard_map/pallas_call | solution.py:122
  2.6 2.2 %collective-permute-start = (f32[144,128]{1,0:T(8,128)}, f32[144,128]{1,0:T(8,128)S(1)}, u32[]{:S(2)}, u32[]{:S(2)}) collective-permute-start(f32[144,128]{1,0:T(8,128)} %get-tuple-element.21), channel_id=1, source_target_pairs={{0,1},{1,2},{2,3},{3,0},{4,5},{5,6},{6,7},{7,4},{8,9},{9,10},{10,1... | collective-permute-start | bytes 221192 | tf_op jit(solution)/shard_map/ppermute | solution.py:602
  4.8 1.5 %collective-permute-start.1 = (f32[144,128]{1,0:T(8,128)}, f32[144,128]{1,0:T(8,128)}, u32[]{:S(2)}, u32[]{:S(2)}) collective-permute-start(f32[144,128]{1,0:T(8,128)} %get-tuple-element.22), channel_id=1, source_target_pairs={{1,0},{2,1},{3,2},{0,3},{5,4},{6,5},{7,6},{4,7},{9,8},{10,9},{11,1... | collective-permute-start | bytes 221192 | tf_op jit(solution)/shard_map/ppermute | solution.py:603
  6.3 2.0 %shard_map.128.table_hbm = f32[128,128]{1,0:T(8,128)} custom-call(s32[192]{0:T(256)} %times.1, s32[12,48]{1,0:T(8,128)} %bitcast.6), custom_call_target="tpu_custom_call" | custom-call | tf_op jit(solution)/shard_map/pallas_call | solution.py:209
  8.3 0.0 collective-permute-done.from_left.left_hbm
  8.3 0.0 copy-start.1
  8.3 0.0 collective-permute-done.1.from_right.right_hbm
  8.3 0.6 copy-done.1
  9.0 1.6 %shard_map.129 = (f32[8,1920]{1,0:T(8,128)}, f32[8,1920]{1,0:T(8,128)}) custom-call(f32[8,1920]{1,0:T(8,128)} %get-tuple-element.25.up_own, f32[8,1920]{1,0:T(8,128)} %get-tuple-element.26.down_own, f32[144,128]{1,0:T(8,128)} %copy-done.1, f32[144,128]{1,0:T(8,128)} %collective-permute-done.1.from_right.right_hbm), custom_call_target="tpu_custom_call", output_to_operand_aliasing={{0}: (0, {}), {1}: (1, {})} | custom-call | tf_op jit(solution)/shard_map/pallas_call | solution.py:174
  10.6 2.8 %collective-permute-start.2 = (f32[8,1920]{1,0:T(8,128)}, f32[8,1920]{1,0:T(8,128)S(1)}, u32[]{:S(2)}, u32[]{:S(2)}) collective-permute-start(f32[8,1920]{1,0:T(8,128)} %get-tuple-element.27), channel_id=1, source_target_pairs={{0,4},{4,8},{8,12},{12,16},{16,20},{20,24},{24,28},{28,32},{32,36}... | collective-permute-start | bytes 184328 | tf_op jit(solution)/shard_map/ppermute | solution.py:602
  13.4 0.0 collective-permute-start.3
  13.4 1.6 %collective-permute-done.2.above_hbm = f32[8,1920]{1,0:T(8,128)S(1)} collective-permute-done((f32[8,1920]{1,0:T(8,128)}, f32[8,1920]{1,0:T(8,128)S(1)}, u32[]{:S(2)}, u32[]{:S(2)}) %collective-permute-start.2) | collective-permute-done | bytes 61472 | tf_op jit(solution)/shard_map/ppermute | solution.py:602
  15.0 0.0 copy-start.2
  15.0 2.5 %collective-permute-done.3.below_hbm = f32[8,1920]{1,0:T(8,128)S(1)} collective-permute-done((f32[8,1920]{1,0:T(8,128)}, f32[8,1920]{1,0:T(8,128)S(1)}, u32[]{:S(2)}, u32[]{:S(2)}) %collective-permute-start.3) | collective-permute-done | bytes 61472 | tf_op jit(solution)/shard_map/ppermute | solution.py:603
  17.5 0.0 copy-start.3
  17.5 0.0 copy-done.2
  17.5 0.6 copy-done.3
  18.1 9.6 %shard_map.130 = (f32[48,1536]{1,0:T(8,128)}, f32[48,1536]{1,0:T(8,128)}, f32[48,1536]{1,0:T(8,128)}, f32[3712,128]{1,0:T(8,128)}) custom-call(s32[12,48]{1,0:T(8,128)} %bitcast.7, s32[12,48]{1,0:T(8,128)} %bitcast.13, f32[48,1536]{1,0:T(8,128)} %u_in.1, f32[48,1536]{1,0:T(8,128)} %h_in.1, f32[48,1536]{1,0:T(8,128)} %a_in.1, f32[144,128]{1,0:T(8,128)} %copy-done.1, ...), custom_call_target="tpu_custom_call" | custom-call | tf_op jit(solution)/shard_map/pallas_call | solution.py:394
  27.8 39.7 %all_to_all.10 = f32[128,1,3712]{2,1,0:T(1,128)} all-to-all(f32[128,1,3712]{2,1,0:T(1,128)} %bitcast.12), channel_id=1, replica_groups=mesh['gz'=32,'gy'=4] {'gz','gy'}, dimensions={0} | all-to-all | bytes 3801088 | tf_op jit(solution)/shard_map/all_to_all | solution.py:609
  67.5 5.6 %shard_map.131 = f32[1792,128]{1,0:T(8,128)} custom-call(f32[3712,128]{1,0:T(8,128)} %bitcast.9, f32[1792,8,128]{2,1,0:T(8,128)} %chain_hbm.3, f32[1792,128]{1,0:T(8,128)} %tension_hbm.3), custom_call_target="tpu_custom_call" | custom-call | flops 36700160 | bytes 7340032 | tf_op jit(solution)/shard_map/pallas_call | solution.py:554
  73.1 0.0 copy-start
  73.1 4.8 %all-to-all-start.1 = ((f32[128,1,1792]{2,1,0:T(1,128)}), f32[128,1,1792]{2,1,0:T(1,128)}, u32[]{:S(2)}, u32[]{:S(2)}) async-start(f32[128,1,1792]{2,1,0:T(1,128)} %bitcast.11), calls=%async_computation.1 | async-start | bytes 1835008 | tf_op jit(solution)/shard_map/all_to_all | solution.py:609
  77.9 7.3 %shard_map.133 = (f32[1792,8,128]{2,1,0:T(8,128)}, f32[1792,128]{1,0:T(8,128)}) custom-call(f32[3712,128]{1,0:T(8,128)} %bitcast.10, f32[1792,8,128]{2,1,0:T(8,128)} %chain_hbm.3, f32[1792,128]{1,0:T(8,128)} %tension_hbm.3), custom_call_target="tpu_custom_call" | custom-call | flops 36700160 | bytes 14680064 | tf_op jit(solution)/shard_map/pallas_call | solution.py:566
  85.2 10.5 %all-to-all-done.1 = f32[128,1,1792]{2,1,0:T(1,128)} async-done(((f32[128,1,1792]{2,1,0:T(1,128)}), f32[128,1,1792]{2,1,0:T(1,128)}, u32[]{:S(2)}, u32[]{:S(2)}) %all-to-all-start.1) | async-done | bytes 917536 | tf_op jit(solution)/shard_map/all_to_all | solution.py:609
  95.8 0.0 copy-done
  95.8 2.6 %shard_map.132 = f32[48,1536]{1,0:T(8,128)} custom-call(s32[12,48]{1,0:T(8,128)S(1)} %bitcast.8, f32[1792,128]{1,0:T(8,128)} %bitcast.5.back), custom_call_target="tpu_custom_call" | custom-call | tf_op jit(solution)/shard_map/pallas_call | solution.py:590
Async XLA Ops:
  2.6 5.8 %collective-permute-start = (f32[144,128]{1,0:T(8,128)}, f32[144,128]{1,0:T(8,128)S(1)}, u32[]{:S(2)}, u32[]{:S(2)}) collective-permute-start(f32[144,128]{1,0:T(8,128)} %get-tuple-element.21), channel_id=1, source_target_pairs={{0,1},{1,2},{2,3},{3,0},{4,5},{5,6},{6,7},{7,4},{8,9},{9,10},{10,1... | collective-permute-start | bytes 221192 | tf_op jit(solution)/shard_map/ppermute | solution.py:602
  4.8 3.6 %collective-permute-start.1 = (f32[144,128]{1,0:T(8,128)}, f32[144,128]{1,0:T(8,128)}, u32[]{:S(2)}, u32[]{:S(2)}) collective-permute-start(f32[144,128]{1,0:T(8,128)} %get-tuple-element.22), channel_id=1, source_target_pairs={{1,0},{2,1},{3,2},{0,3},{5,4},{6,5},{7,6},{4,7},{9,8},{10,9},{11,1... | collective-permute-start | bytes 221192 | tf_op jit(solution)/shard_map/ppermute | solution.py:603
  8.3 0.6 copy-start.1
  10.6 4.4 %collective-permute-start.2 = (f32[8,1920]{1,0:T(8,128)}, f32[8,1920]{1,0:T(8,128)S(1)}, u32[]{:S(2)}, u32[]{:S(2)}) collective-permute-start(f32[8,1920]{1,0:T(8,128)} %get-tuple-element.27), channel_id=1, source_target_pairs={{0,4},{4,8},{8,12},{12,16},{16,20},{20,24},{24,28},{28,32},{32,36}... | collective-permute-start | bytes 184328 | tf_op jit(solution)/shard_map/ppermute | solution.py:602
  13.4 4.2 %collective-permute-start.3 = (f32[8,1920]{1,0:T(8,128)}, f32[8,1920]{1,0:T(8,128)S(1)}, u32[]{:S(2)}, u32[]{:S(2)}) collective-permute-start(f32[8,1920]{1,0:T(8,128)} %get-tuple-element.28), channel_id=1, source_target_pairs={{4,0},{8,4},{12,8},{16,12},{20,16},{24,20},{28,24},{32,28},{36,32}... | collective-permute-start | bytes 184328 | tf_op jit(solution)/shard_map/ppermute | solution.py:603
  15.0 2.5 %copy-start.2 = (f32[8,1920]{1,0:T(8,128)}, f32[8,1920]{1,0:T(8,128)S(1)}, u32[]{:S(2)}) copy-start(f32[8,1920]{1,0:T(8,128)S(1)} %collective-permute-done.2.above_hbm) | copy-start | bytes 184324
  17.5 0.6 copy-start.3
  73.1 22.7 %copy-start = (s32[48,12]{0,1:T(8,128)S(1)}, s32[48,12]{0,1:T(8,128)}, u32[]{:S(2)}) copy-start(s32[48,12]{0,1:T(8,128)} %param.12) | copy-start | bytes 6916
  73.1 22.7 %all-to-all-start.1 = ((f32[128,1,1792]{2,1,0:T(1,128)}), f32[128,1,1792]{2,1,0:T(1,128)}, u32[]{:S(2)}, u32[]{:S(2)}) async-start(f32[128,1,1792]{2,1,0:T(1,128)} %bitcast.11), calls=%async_computation.1 | async-start | bytes 1835008 | tf_op jit(solution)/shard_map/all_to_all | solution.py:609

commit v5 on v4

--- a/solution.py
+++ b/solution.py
@@ -84,7 +84,7 @@
     return jnp.where(row < 3, u, jnp.where(row < 6, h, a))
 
 
-def pack_y_kernel(u, h, a, to_left, to_right, up, down, left, right, ends, sems):
+def pack_y_kernel(u, h, a, to_left, to_right, own, left, right, ends, sems):
     wide = 2 * LANES
     pairs = []
     for f, field in enumerate((u, h, a)):
@@ -94,10 +94,8 @@
         pairs.append((field.at[ROWS - 8 : ROWS, :], ends.at[1, f]))
     for copy in start_all(pairs, sems):
         copy.wait()
-    for out, e, (_, shifts) in zip((up, down), (0, 1), Z_SHIFTS):
-        zero = jnp.zeros((8, LANES), F32)
-        out[:, 0:LANES], out[:, LANES:OWN], out[:, OWN + COLS : WIDE] = zero, zero, zero
-        out[:, OWN : OWN + COLS] = three_fields([ends[e, f] for f in range(3)], shifts)
+    for e, (_, shifts) in enumerate(Z_SHIFTS):
+        own[8 * e : 8 * e + 8, :] = three_fields([ends[e, f] for f in range(3)], shifts)
     lane = lanes_of((ROWS, LANES))
     first, second = slice(0, LANES), slice(LANES, wide)
     to_left[0:ROWS, :] = left[0, :, first]
@@ -118,12 +116,12 @@
 
 def pack_y(u, h, a):
     shape = jax.ShapeDtypeStruct((3 * ROWS, LANES), F32)
-    rows = jax.ShapeDtypeStruct((8, WIDE), F32)
+    rows = jax.ShapeDtypeStruct((16, COLS), F32)
     return pl.pallas_call(
         pack_y_kernel,
-        out_shape=(shape, shape, rows, rows),
+        out_shape=(shape, shape, rows),
         in_specs=[HBM] * 3,
-        out_specs=[VMEM] * 4,
+        out_specs=[VMEM] * 3,
         scratch_shapes=[
             pltpu.VMEM((3, ROWS, 2 * LANES), F32),
             pltpu.VMEM((3, ROWS, 2 * LANES), F32),
@@ -157,29 +155,23 @@
     )
 
 
-def pack_z_kernel(up_own, down_own, from_left, from_right, up, down, edges, sems):
-    pairs = []
+def pack_z_kernel(own, from_left, from_right, up, down):
     for e, (out, (lo, shifts)) in enumerate(zip((up, down), Z_SHIFTS)):
         sides = side_tiles(from_left, from_right, lo, 8)
-        for t in range(3):
-            edges[e, :, t * LANES : (t + 1) * LANES] = three_fields([side[t] for side in sides], shifts)
-        pairs.append((edges.at[e, :, 0:OWN], out.at[:, 0:OWN]))
-        pairs.append((edges.at[e, :, OWN : 3 * LANES], out.at[:, OWN + COLS : WIDE]))
-    for copy in start_all(pairs, sems):
-        copy.wait()
-
-
-def pack_z(up_own, down_own, from_left, from_right):
+        out[:, OWN : OWN + COLS] = own[8 * e : 8 * e + 8, :]
+        for t, at in enumerate((0, LANES, OWN + COLS)):
+            out[:, at : at + LANES] = three_fields([side[t] for side in sides], shifts)
+
+
+def pack_z(own, from_left, from_right):
     shape = jax.ShapeDtypeStruct((8, WIDE), F32)
     return pl.pallas_call(
         pack_z_kernel,
         out_shape=(shape, shape),
-        in_specs=[HBM, HBM, VMEM, VMEM],
-        out_specs=(HBM, HBM),
-        input_output_aliases={0: 0, 1: 1},
-        scratch_shapes=[pltpu.VMEM((2, 8, 3 * LANES), F32), pltpu.SemaphoreType.DMA((4,))],
-        compiler_params=whole_grant(200 * 2**10),
-    )(up_own, down_own, from_left, from_right)
+        in_specs=[VMEM] * 3,
+        out_specs=(VMEM, VMEM),
+        compiler_params=grant(4),
+    )(own, from_left, from_right)
 
 
 def table_kernel(times, keeper, table):
@@ -611,11 +603,11 @@
 
 def body(u, h, a, tally, keeper, times, chain, tension):
     tally, keeper = tally.T, keeper.T
-    to_left, to_right, up_own, down_own = pack_y(u, h, a)
+    to_left, to_right, own = pack_y(u, h, a)
     from_left, from_right = both_ways("gy", to_left, to_right)
     table = solid_table(times, keeper)
-    up_own, down_own, table = lax.optimization_barrier((up_own, down_own, table))
-    up, down = pack_z(up_own, down_own, from_left, from_right)
+    own, table, from_left, from_right = lax.optimization_barrier((own, table, from_left, from_right))
+    up, down = pack_z(own, from_left, from_right)
     above, below = both_ways("gz", up, down)
     t_new, h_new, m_new, send = sweeps(keeper, tally, u, h, a, from_left, from_right, above, below, table)
     got = exchange(send)

time: 98.9 us -> 98 us (level)
  Pallas kernels: 30.8 us -> 29.3 us
    pallas_call x2, Pallas kernels: 3.57 us -> 2.03 us  [the longest x1 1.94 us: pack_y(): pl.pallas_call(pack_y_kernel, out_shape=(shape, shape, rows), in_specs=[H...]
where the time goes in v5:
time: 98 us; the launch traced here: 97.4 us
  blocking collectives  39.8 us (41%)
  Pallas kernels  29.3 us (30%)
  waiting for transfers between devices  14.5 us (15%)
  starting transfers between devices  11.6 us (12%)
  local copies, waits for them, and re-layouts  1.57 us (2%)
    all_to_all x1, blocking collectives, exchange(): lax.all_to_all(flat, ('gz', 'gy'), split_axis=0, concat_axis=0, tiled=True)  39.8 us
    all_to_all x1, waiting for transfers between devices, exchange(): lax.all_to_all(flat, ('gz', 'gy'), split_axis=0, concat_axis=0, tiled=True)  10.5 us
    pallas_call x1, Pallas kernels, sweeps(): pl.pallas_call(sweep_kernel, out_shape=(grid_shape, grid_shape, grid_shap...  9.64 us
    pallas_call x1, Pallas kernels, states_of(): pl.pallas_call(state_kernel, out_shape=(jax.ShapeDtypeStruct(chain.shape,...  7.33 us
    pallas_call x1, Pallas kernels, creep_of(): pl.pallas_call(creep_kernel, out_shape=jax.ShapeDtypeStruct(shape, F32),...  5.64 us
    ppermute x2, starting transfers between devices, both_ways(): lax.ppermute(to_higher, axis, [(i, (i + 1) % count) for i in range(count)])  5.27 us
    all_to_all x1, starting transfers between devices, exchange(): lax.all_to_all(flat, ('gz', 'gy'), split_axis=0, concat_axis=0, tiled=True)  4.77 us
    ppermute x2, waiting for transfers between devices, both_ways(): lax.ppermute(to_lower, axis, [((i + 1) % count, i) for i in range(count)])  2.65 us
  transfers between devices with their start and end apart: 5, of which 3 were waited for; matrix products, arithmetic and copies ran while one was open for 0% of the time, Pallas kernels for 10%

profile of v5, /device:TPU:1, one launch (start us, length us, event | category | flops | bytes accessed | tf_op | source)
XLA Modules:
  0.0 97.4 jit_solution(16981602176225769210)
XLA Ops:
  0.6 1.9 %shard_map.127 = (f32[144,128]{1,0:T(8,128)}, f32[144,128]{1,0:T(8,128)}, f32[16,1536]{1,0:T(8,128)}) custom-call(f32[48,1536]{1,0:T(8,128)} %u_in.1, f32[48,1536]{1,0:T(8,128)} %h_in.1, f32[48,1536]{1,0:T(8,128)} %a_in.1), custom_call_target="tpu_custom_call" | custom-call | tf_op jit(solution)/shard_map/pallas_call | solution.py:120
  2.6 2.2 %collective-permute-start = (f32[144,128]{1,0:T(8,128)}, f32[144,128]{1,0:T(8,128)S(1)}, u32[]{:S(2)}, u32[]{:S(2)}) collective-permute-start(f32[144,128]{1,0:T(8,128)} %get-tuple-element.22), channel_id=1, source_target_pairs={{0,1},{1,2},{2,3},{3,0},{4,5},{5,6},{6,7},{7,4},{8,9},{9,10},{10,1... | collective-permute-start | bytes 221192 | tf_op jit(solution)/shard_map/ppermute | solution.py:594
  4.8 1.5 %collective-permute-start.1 = (f32[144,128]{1,0:T(8,128)}, f32[144,128]{1,0:T(8,128)S(1)}, u32[]{:S(2)}, u32[]{:S(2)}) collective-permute-start(f32[144,128]{1,0:T(8,128)} %get-tuple-element.23), channel_id=1, source_target_pairs={{1,0},{2,1},{3,2},{0,3},{5,4},{6,5},{7,6},{4,7},{9,8},{10,9},{11,1... | collective-permute-start | bytes 221192 | tf_op jit(solution)/shard_map/ppermute | solution.py:595
  6.3 2.0 %shard_map.128.table_hbm = f32[128,128]{1,0:T(8,128)} custom-call(s32[192]{0:T(256)} %times.1, s32[12,48]{1,0:T(8,128)} %bitcast.6), custom_call_target="tpu_custom_call" | custom-call | tf_op jit(solution)/shard_map/pallas_call | solution.py:201
  8.3 0.0 collective-permute-done.from_left.left_hbm
  8.3 0.0 copy-start
  8.3 0.0 collective-permute-done.1.from_right.right_hbm
  8.3 0.0 copy-start.1
  8.3 0.0 copy-start.2
  8.3 0.9 copy-done.2
  9.3 0.1 shard_map.129
  9.4 3.1 %collective-permute-start.2 = (f32[8,1920]{1,0:T(8,128)S(1)}, f32[8,1920]{1,0:T(8,128)S(1)}, u32[]{:S(2)}, u32[]{:S(2)}) collective-permute-start(f32[8,1920]{1,0:T(8,128)S(1)} %get-tuple-element.27), channel_id=1, source_target_pairs={{0,4},{4,8},{8,12},{12,16},{16,20},{20,24},{24,28},{28,32},{32,36}... | collective-permute-start | bytes 184328 | tf_op jit(solution)/shard_map/ppermute | solution.py:594
  12.5 0.0 collective-permute-start.3
  12.5 1.3 %collective-permute-done.2.above_hbm = f32[8,1920]{1,0:T(8,128)S(1)} collective-permute-done((f32[8,1920]{1,0:T(8,128)S(1)}, f32[8,1920]{1,0:T(8,128)S(1)}, u32[]{:S(2)}, u32[]{:S(2)}) %collective-permute-start.2) | collective-permute-done | bytes 61472 | tf_op jit(solution)/shard_map/ppermute | solution.py:594
  13.7 0.0 copy-start.4
  13.7 2.6 %collective-permute-done.3.below_hbm = f32[8,1920]{1,0:T(8,128)S(1)} collective-permute-done((f32[8,1920]{1,0:T(8,128)S(1)}, f32[8,1920]{1,0:T(8,128)S(1)}, u32[]{:S(2)}, u32[]{:S(2)}) %collective-permute-start.3) | collective-permute-done | bytes 61472 | tf_op jit(solution)/shard_map/ppermute | solution.py:595
  16.4 0.0 copy-start.5
  16.4 0.0 copy-done
  16.4 0.0 copy-done.1
  16.4 0.0 copy-done.4
  16.4 0.6 copy-done.5
  17.0 9.6 %shard_map.130 = (f32[48,1536]{1,0:T(8,128)}, f32[48,1536]{1,0:T(8,128)}, f32[48,1536]{1,0:T(8,128)}, f32[3712,128]{1,0:T(8,128)}) custom-call(s32[12,48]{1,0:T(8,128)} %bitcast.7, s32[12,48]{1,0:T(8,128)} %bitcast.13, f32[48,1536]{1,0:T(8,128)} %u_in.1, f32[48,1536]{1,0:T(8,128)} %h_in.1, f32[48,1536]{1,0:T(8,128)} %a_in.1, f32[144,128]{1,0:T(8,128)} %copy-done, ...), custom_call_target="tpu_custom_call" | custom-call | tf_op jit(solution)/shard_map/pallas_call | solution.py:386
  26.7 39.8 %all_to_all.10 = f32[128,1,3712]{2,1,0:T(1,128)} all-to-all(f32[128,1,3712]{2,1,0:T(1,128)} %bitcast.12), channel_id=1, replica_groups=mesh['gz'=32,'gy'=4] {'gz','gy'}, dimensions={0} | all-to-all | bytes 3801088 | tf_op jit(solution)/shard_map/all_to_all | solution.py:601
  66.5 5.6 %shard_map.131 = f32[1792,128]{1,0:T(8,128)} custom-call(f32[3712,128]{1,0:T(8,128)} %bitcast.9, f32[1792,8,128]{2,1,0:T(8,128)} %chain_hbm.3, f32[1792,128]{1,0:T(8,128)} %tension_hbm.3), custom_call_target="tpu_custom_call" | custom-call | flops 36700160 | bytes 7340032 | tf_op jit(solution)/shard_map/pallas_call | solution.py:546
  72.2 0.0 copy-start.3
  72.2 4.8 %all-to-all-start.1 = ((f32[128,1,1792]{2,1,0:T(1,128)}), f32[128,1,1792]{2,1,0:T(1,128)}, u32[]{:S(2)}, u32[]{:S(2)}) async-start(f32[128,1,1792]{2,1,0:T(1,128)} %bitcast.11), calls=%async_computation.1 | async-start | bytes 1835008 | tf_op jit(solution)/shard_map/all_to_all | solution.py:601
  76.9 7.3 %shard_map.133 = (f32[1792,8,128]{2,1,0:T(8,128)}, f32[1792,128]{1,0:T(8,128)}) custom-call(f32[3712,128]{1,0:T(8,128)} %bitcast.10, f32[1792,8,128]{2,1,0:T(8,128)} %chain_hbm.3, f32[1792,128]{1,0:T(8,128)} %tension_hbm.3), custom_call_target="tpu_custom_call" | custom-call | flops 36700160 | bytes 14680064 | tf_op jit(solution)/shard_map/pallas_call | solution.py:558
  84.3 10.5 %all-to-all-done.1 = f32[128,1,1792]{2,1,0:T(1,128)} async-done(((f32[128,1,1792]{2,1,0:T(1,128)}), f32[128,1,1792]{2,1,0:T(1,128)}, u32[]{:S(2)}, u32[]{:S(2)}) %all-to-all-start.1) | async-done | bytes 917536 | tf_op jit(solution)/shard_map/all_to_all | solution.py:601
  94.8 0.0 copy-done.3
  94.8 2.6 %shard_map.132 = f32[48,1536]{1,0:T(8,128)} custom-call(s32[12,48]{1,0:T(8,128)S(1)} %bitcast.8, f32[1792,128]{1,0:T(8,128)} %bitcast.5.back), custom_call_target="tpu_custom_call" | custom-call | tf_op jit(solution)/shard_map/pallas_call | solution.py:582
Async XLA Ops:
  2.6 5.7 %collective-permute-start = (f32[144,128]{1,0:T(8,128)}, f32[144,128]{1,0:T(8,128)S(1)}, u32[]{:S(2)}, u32[]{:S(2)}) collective-permute-start(f32[144,128]{1,0:T(8,128)} %get-tuple-element.22), channel_id=1, source_target_pairs={{0,1},{1,2},{2,3},{3,0},{4,5},{5,6},{6,7},{7,4},{8,9},{9,10},{10,1... | collective-permute-start | bytes 221192 | tf_op jit(solution)/shard_map/ppermute | solution.py:594
  4.8 3.5 %collective-permute-start.1 = (f32[144,128]{1,0:T(8,128)}, f32[144,128]{1,0:T(8,128)S(1)}, u32[]{:S(2)}, u32[]{:S(2)}) collective-permute-start(f32[144,128]{1,0:T(8,128)} %get-tuple-element.23), channel_id=1, source_target_pairs={{1,0},{2,1},{3,2},{0,3},{5,4},{6,5},{7,6},{4,7},{9,8},{10,9},{11,1... | collective-permute-start | bytes 221192 | tf_op jit(solution)/shard_map/ppermute | solution.py:595
  8.3 8.1 %copy-start = (f32[144,128]{1,0:T(8,128)}, f32[144,128]{1,0:T(8,128)S(1)}, u32[]{:S(2)}) copy-start(f32[144,128]{1,0:T(8,128)S(1)} %collective-permute-done.from_left.left_hbm) | copy-start | bytes 221188
  8.3 8.1 %copy-start.1 = (f32[144,128]{1,0:T(8,128)}, f32[144,128]{1,0:T(8,128)S(1)}, u32[]{:S(2)}) copy-start(f32[144,128]{1,0:T(8,128)S(1)} %collective-permute-done.1.from_right.right_hbm) | copy-start | bytes 221188
  8.3 1.0 copy-start.2
  9.4 4.4 %collective-permute-start.2 = (f32[8,1920]{1,0:T(8,128)S(1)}, f32[8,1920]{1,0:T(8,128)S(1)}, u32[]{:S(2)}, u32[]{:S(2)}) collective-permute-start(f32[8,1920]{1,0:T(8,128)S(1)} %get-tuple-element.27), channel_id=1, source_target_pairs={{0,4},{4,8},{8,12},{12,16},{16,20},{20,24},{24,28},{28,32},{32,36}... | collective-permute-start | bytes 184328 | tf_op jit(solution)/shard_map/ppermute | solution.py:594
  12.5 3.9 %collective-permute-start.3 = (f32[8,1920]{1,0:T(8,128)S(1)}, f32[8,1920]{1,0:T(8,128)S(1)}, u32[]{:S(2)}, u32[]{:S(2)}) collective-permute-start(f32[8,1920]{1,0:T(8,128)S(1)} %get-tuple-element.28), channel_id=1, source_target_pairs={{4,0},{8,4},{12,8},{16,12},{20,16},{24,20},{28,24},{32,28},{36,32}... | collective-permute-start | bytes 184328 | tf_op jit(solution)/shard_map/ppermute | solution.py:595
  13.7 2.7 %copy-start.4 = (f32[8,1920]{1,0:T(8,128)}, f32[8,1920]{1,0:T(8,128)S(1)}, u32[]{:S(2)}) copy-start(f32[8,1920]{1,0:T(8,128)S(1)} %collective-permute-done.2.above_hbm) | copy-start | bytes 184324
  16.4 0.6 copy-start.5
  72.2 22.7 %copy-start.3 = (s32[48,12]{0,1:T(8,128)S(1)}, s32[48,12]{0,1:T(8,128)}, u32[]{:S(2)}) copy-start(s32[48,12]{0,1:T(8,128)} %param.12) | copy-start | bytes 6916
  72.2 22.7 %all-to-all-start.1 = ((f32[128,1,1792]{2,1,0:T(1,128)}), f32[128,1,1792]{2,1,0:T(1,128)}, u32[]{:S(2)}, u32[]{:S(2)}) async-start(f32[128,1,1792]{2,1,0:T(1,128)} %bitcast.11), calls=%async_computation.1 | async-start | bytes 1835008 | tf_op jit(solution)/shard_map/all_to_all | solution.py:601
